TPU v7x, 512 devices: a whole 4x4x16 slice. The times are simulated.
512 devices in a mesh: dp: 8 (over x, core), graph: 64 (over z, y).
Axes of the slice: x: 4, y: 4, z: 16, core: 2. Of those that a mesh axis runs over, the one named last changes fastest.
Arguments:
- edge_state: bfloat16 [524288, 512], P(('dp', 'graph')), parts along dimension 0, may hold values from -6 to 6
- cotangent: bfloat16 [524288, 512], P(('dp', 'graph')), parts along dimension 0, may hold values from -6 to 6
- basis_values: bfloat16 [42, 4194304], P(None, ('dp', 'graph')), parts along dimension 1, may hold values from -5 to 5
- down_weight: bfloat16 [512, 64], replicated, may hold values from -0.25 to 0.25
- basis_weight: bfloat16 [42, 64], replicated, may hold values from -1 to 1
- up_weight: bfloat16 [64, 512], replicated, may hold values from -0.75 to 0.75
- triplet_source: int32 [4194304], P(('dp', 'graph')), parts along dimension 0, may hold values from 0 to 1279, as said below
- triplet_target: int32 [4194304], P(('dp', 'graph')), parts along dimension 0, may hold values from 0 to 1023
- block_valid: int32 [65536], P(('dp', 'graph')), parts along dimension 0, may hold values from 1 to 64, as said below
- send_lists: int32 [2048, 64], P(('dp', 'graph')), parts along dimension 0, may hold values from 0 to 1023, as said below
Outputs:
- edge_grad: bfloat16 [524288, 512], P(('dp', 'graph')), parts along dimension 0
- grad_down: float32 [4096, 64], P('dp'), parts along dimension 0
- grad_basis: float32 [336, 64], P('dp'), parts along dimension 0
- grad_up: float32 [512, 512], P('dp'), parts along dimension 0
There are 8 independent parts, one for each index of `dp`. A program takes and returns all parts, laid end to end along the dimension named above; an argument that names none is the same for every part. Nothing has to cross between parts.
Inputs may be any that keep to these rules, and one draw needn't show every extreme that they name: `triplet_source`: for a triplet owned by device d: values below 1024 name d's own edges; value 1024 + k * 64 + r names row r of the block that device d + o_k sends to d, and only devices that exist are named. `block_valid`: the first block of every device is full. `send_lists`: row d * 4 + k lists local edge numbers of device d, sent to device d - o_k.
All inputs are finite; a program needn't handle non-finite values.
Results may differ from a plain program's by a relative error of at most 0.0077.
Values may be sent and summed in bfloat16 or wider, within the bound.
A program may use at most 64 MiB of HBM per device.

v0:
```python
import jax
import jax.numpy as jnp
from jax import lax
from jax.sharding import PartitionSpec as P

TRIP_BLOCK = 64


residual_scale = 0.7071067811865476
neighbour_offsets = (-2, -1, 1, 2)


def shifted(value, axis, steps):
    count = lax.axis_size(axis)
    initial, last = (max(0, -steps), min(count, count - steps))
    return lax.ppermute(value, axis, [(source, source + steps) for source in range(initial, last)])


def silu_slope(value):
    sigma = jax.nn.sigmoid(value)
    return sigma * (1.0 + value * (1.0 - sigma))


def per_device(
    edge_state,
    cotangent,
    basis_values,
    down_weight,
    basis_weight,
    up_weight,
    triplet_source,
    triplet_target,
    block_valid,
    send_lists,
):
    edge_count = edge_state.shape[0]
    width = down_weight.shape[1]
    peer_count = len(neighbour_offsets)
    contract_rows = (((0,), (0,)), ((), ()))
    contract_cols = (((1,), (1,)), ((), ()))
    projected = jnp.dot(edge_state, down_weight, preferred_element_type=jnp.float32)
    hidden = jax.nn.silu(projected).astype(jnp.bfloat16)
    slot_rows = send_lists.shape[1]
    outgoing = edge_state[send_lists]
    received = []
    for slot_index in range(peer_count):
        offset = neighbour_offsets[slot_index]
        received.append(shifted(outgoing[slot_index], "graph", -offset))
    remote_state = jnp.concatenate(received, axis=0)
    remote_hidden = jax.nn.silu(
        jnp.dot(remote_state, down_weight, preferred_element_type=jnp.float32)
    ).astype(jnp.bfloat16)
    table = jnp.concatenate([hidden, remote_hidden], axis=0)
    source_rows = table[triplet_source]
    basis = lax.dot_general(
        basis_values, basis_weight, contract_rows, preferred_element_type=jnp.float32
    )
    position = jnp.arange(triplet_source.shape[0], dtype=jnp.int32)
    valid = (position % TRIP_BLOCK < jnp.repeat(block_valid, TRIP_BLOCK)).astype(jnp.float32)[
        :, None
    ]
    message = valid * source_rows.astype(jnp.float32) * basis
    aggregate = jax.ops.segment_sum(message, triplet_target, num_segments=edge_count).astype(
        jnp.bfloat16
    )
    up_input = jnp.dot(aggregate, up_weight, preferred_element_type=jnp.float32)
    up_grad = (cotangent.astype(jnp.float32) * residual_scale * silu_slope(up_input)).astype(
        jnp.bfloat16
    )
    grad_up = lax.dot_general(aggregate, up_grad, contract_rows, preferred_element_type=jnp.float32)
    target_grad = lax.dot_general(
        up_grad, up_weight, contract_cols, preferred_element_type=jnp.float32
    ).astype(jnp.bfloat16)
    gate = valid * target_grad[triplet_target].astype(jnp.float32)
    source_grad = gate * basis
    basis_grad = (gate * source_rows.astype(jnp.float32)).astype(jnp.bfloat16)
    grad_basis = jnp.dot(basis_values, basis_grad, preferred_element_type=jnp.float32)
    table_grad = jax.ops.segment_sum(source_grad, triplet_source, num_segments=table.shape[0])
    returning = table_grad[edge_count:].reshape(peer_count, slot_rows, width)
    backs = []
    for slot_index in range(peer_count):
        offset = neighbour_offsets[slot_index]
        backs.append(shifted(returning[slot_index], "graph", offset))
    returned = jnp.concatenate(backs, axis=0)
    remote_grad = jax.ops.segment_sum(returned, send_lists.reshape(-1), num_segments=edge_count)
    hidden_grad = table_grad[:edge_count] + remote_grad
    gate_grad = (hidden_grad * silu_slope(projected)).astype(jnp.bfloat16)
    grad_down = lax.dot_general(
        edge_state, gate_grad, contract_rows, preferred_element_type=jnp.float32
    )
    through_down = lax.dot_general(
        gate_grad, down_weight, contract_cols, preferred_element_type=jnp.float32
    )
    edge_grad = (cotangent.astype(jnp.float32) * residual_scale + through_down).astype(jnp.bfloat16)
    grad_down, grad_basis, grad_up = lax.psum((grad_down, grad_basis, grad_up), "graph")
    return (edge_grad, grad_down, grad_basis, grad_up)


def solution(mesh):
    return jax.shard_map(
        per_device,
        mesh=mesh,
        in_specs=(
            P(("dp", "graph"), None),
            P(("dp", "graph"), None),
            P(None, ("dp", "graph")),
            P(),
            P(),
            P(),
            P(("dp", "graph")),
            P(("dp", "graph")),
            P(("dp", "graph")),
            P(("dp", "graph"), None),
        ),
        out_specs=(P(("dp", "graph"), None), P("dp", None), P("dp", None), P("dp", None)),
        check_vma=False,
    )
```

profile of v0, /device:TPU:6, one launch (start us, length us, event | category | flops | bytes accessed | tf_op | source)
XLA Modules:
  0.0 770.9 jit_solution(16507255383061321428)
XLA Ops:
  9.6 5.1 collective-permute-start
  16.0 4.5 collective-permute-start.1
  24.0 4.3 collective-permute-done.3
  28.7 27.9 %gather_fusion.1 = bf16[8192,64]{1,0:T(8,128)(2,1)S(1)} fusion(bf16[1280,64]{1,0:T(8,128)(2,1)S(1)} %copy.18, s32[8192]{0:T(1024)} %fusion.31), kind=kCustom, calls=%fused_computation.1 | custom fusion | bytes 2129920 | tf_op jit(solution)/shard_map/gather | solution.py:54
  56.6 1.6 copy.19
  58.3 3.3 fusion
  61.6 2.7 copy.20
  64.3 44.4 %scatter_custom_fusion = f32[1024,64]{1,0:T(8,128)S(1)} fusion(s32[8192]{0:T(1024)} %param.17, f32[8192,64]{1,0:T(8,128)} %copy.20, f32[]{:T(128)} %constant.13.clone.1), kind=kCustom, calls=%fused_computation.32 | custom fusion | flops 524288 | bytes 262656 | tf_op jit(solution)/shard_map/scatter-add | solution.py:63
  108.7 2.4 multiply_convert_fusion
  112.8 24.0 %gather_fusion.2 = bf16[8192,64]{1,0:T(8,128)(2,1)S(1)} fusion(bf16[1024,64]{1,0:T(8,128)(2,1)S(1)} %copy.21, s32[8192]{0:T(1024)S(1)} %fusion.32), kind=kCustom, calls=%fused_computation.2 | custom fusion | bytes 2129920 | tf_op jit(solution)/shard_map/gather | solution.py:74
  136.8 1.6 copy.22
  138.4 3.0 convolution_bitcast_fusion.1
  141.4 1.5 fusion.2
  142.9 2.7 copy.23
  145.7 44.5 %scatter_custom_fusion.1 = f32[1280,64]{1,0:T(8,128)S(1)} fusion(s32[8192]{0:T(1024)} %param.16, f32[8192,64]{1,0:T(8,128)} %copy.23, f32[]{:T(128)} %constant.13.clone.1), kind=kCustom, calls=%fused_computation.19 | custom fusion | flops 524288 | bytes 328192 | tf_op jit(solution)/shard_map/scatter-add | solution.py:78
  192.1 6.7 collective-permute-start.7
  198.7 5.3 collective-permute-start.6
  205.4 2.4 fusion.25
  207.8 282.8 %psum.22 = f32[42,64]{1,0:T(8,128)} all-reduce(f32[42,64]{1,0:T(8,128)} %convolution_bitcast_fusion.1), channel_id=1, replica_groups=mesh['dp'=8,'graph'=64] {'graph'}, use_global_device_ids=true, to_apply=%region_4.5 | all-reduce | flops 2688 | bytes 21504 | tf_op jit(solution)/shard_map/psum | solution.py:95
  490.6 2.4 scatter_custom_fusion.2
  494.4 1.4 add_convert_fusion
  495.8 265.1 %all-reduce.3.cloned.1.call-done = (f32[512,64]{0,1:T(8,128)}, f32[64,512]{1,0:T(8,128)}) async-done(((f32[512,64]{0,1:T(8,128)}, f32[64,512]{1,0:T(8,128)}), (f32[512,64]{0,1:T(8,128)}, f32[64,512]{1,0:T(8,128)})) %all-reduce.3.cloned.1.call-update) | async-done | bytes 262160 | tf_op jit(solution)/shard_map/psum | solution.py:95
  760.9 1.6 copy.28
  762.5 1.6 copy.29
  (63 shorter events, 13.8 us)
Async XLA Ops:
  7.2 1.2 copy-start
  7.2 14.7 %copy-start.10 = (s32[8192]{0:T(1024)S(1)}, s32[8192]{0:T(1024)}, u32[]{:S(2)}) copy-start(s32[8192]{0:T(1024)} %param.16) | copy-start | bytes 98308
  7.2 15.3 %copy-start.9 = (s32[8192]{0:T(1024)S(1)}, s32[8192]{0:T(1024)}, u32[]{:S(2)}) copy-start(s32[8192]{0:T(1024)} %param.17) | copy-start | bytes 98308
  7.2 15.3 %copy-start.13 = (s32[128]{0:T(128)S(1)}, s32[128]{0:T(128)}, u32[]{:S(2)}) copy-start(s32[128]{0:T(128)} %param.18) | copy-start | bytes 1540
  7.2 15.5 %copy-start.7 = (bf16[512,64]{0,1:T(8,128)(2,1)S(1)}, bf16[512,64]{0,1:T(8,128)(2,1)}, u32[]{:S(2)}) copy-start(bf16[512,64]{0,1:T(8,128)(2,1)} %param.13) | copy-start | bytes 196612
  7.2 753.7 %all-reduce.3.cloned.1.call-start = ((), (), s32[]{:S(2)}) async-start(), calls=%async_computation | async-start | bytes 524288 | tf_op jit(solution)/shard_map/psum | solution.py:95
  8.4 15.5 %copy-start.12 = (s32[4,64]{1,0:T(4,128)S(1)}, s32[4,64]{1,0:T(4,128)}, u32[]{:S(2)}) copy-start(s32[4,64]{1,0:T(4,128)} %param.19) | copy-start | bytes 3076
  9.6 14.4 %collective-permute-start = (bf16[64,512]{1,0:T(8,128)(2,1)S(1)}, bf16[64,512]{1,0:T(8,128)(2,1)S(1)}, u32[]{:S(2)}, u32[]{:S(2)}) collective-permute-start(bf16[64,512]{1,0:T(8,128)(2,1)S(1)} %get-tuple-element.10), channel_id=1, source_target_pairs={{0,2},{1,3},{2,4},{3,5},{4,6},{5,7},{6,8},{7,9},{8,10},{9,11},{10,... | collective-permute-start | bytes 196616 | tf_op jit(solution)/shard_map/ppermute | solution.py:16
  14.7 9.3 %collective-permute-start.2 = (bf16[64,512]{1,0:T(8,128)(2,1)S(1)}, bf16[64,512]{1,0:T(8,128)(2,1)S(1)}, u32[]{:S(2)}, u32[]{:S(2)}) collective-permute-start(bf16[64,512]{1,0:T(8,128)(2,1)S(1)} %get-tuple-element.11), channel_id=1, source_target_pairs={{1,0},{2,1},{3,2},{4,3},{5,4},{6,5},{7,6},{8,7},{9,8},{10,9},{11,1... | collective-permute-start | bytes 196616 | tf_op jit(solution)/shard_map/ppermute | solution.py:16
  16.0 8.0 %collective-permute-start.1 = (bf16[64,512]{1,0:T(8,128)(2,1)S(1)}, bf16[64,512]{1,0:T(8,128)(2,1)S(1)}, u32[]{:S(2)}, u32[]{:S(2)}) collective-permute-start(bf16[64,512]{1,0:T(8,128)(2,1)S(1)} %get-tuple-element.12), channel_id=1, source_target_pairs={{0,1},{1,2},{2,3},{3,4},{4,5},{5,6},{6,7},{7,8},{8,9},{9,10},{10,1... | collective-permute-start | bytes 196616 | tf_op jit(solution)/shard_map/ppermute | solution.py:16
  20.6 7.7 collective-permute-start.3
  56.6 1.6 copy-start.11
  61.6 47.2 %copy-start.6 = (bf16[64,512]{1,0:T(8,128)(2,1)S(1)}, bf16[64,512]{1,0:T(8,128)(2,1)}, u32[]{:S(2)}) copy-start(bf16[64,512]{1,0:T(8,128)(2,1)} %param.15) | copy-start | bytes 196612
  108.7 2.4 copy-start.3
  111.1 1.0 copy-start.2
  138.4 3.0 copy-start.1
  190.8 299.8 %collective-permute-start.4 = (f32[64,64]{1,0:T(8,128)}, f32[64,64]{1,0:T(8,128)}, u32[]{:S(2)}, u32[]{:S(2)}) collective-permute-start(f32[64,64]{1,0:T(8,128)} %get-tuple-element.6), channel_id=1, source_target_pairs={{2,0},{3,1},{4,2},{5,3},{6,4},{7,5},{8,6},{9,7},{10,8},{11,9},{12,... | collective-permute-start | bytes 49160 | tf_op jit(solution)/shard_map/ppermute | solution.py:16
  192.1 298.5 %collective-permute-start.7 = (f32[64,64]{1,0:T(8,128)}, f32[64,64]{1,0:T(8,128)}, u32[]{:S(2)}, u32[]{:S(2)}) collective-permute-start(f32[64,64]{1,0:T(8,128)} %get-tuple-element.7), channel_id=1, source_target_pairs={{0,2},{1,3},{2,4},{3,5},{4,6},{5,7},{6,8},{7,9},{8,10},{9,11},{10,... | collective-permute-start | bytes 49160 | tf_op jit(solution)/shard_map/ppermute | solution.py:16
  198.7 291.9 %collective-permute-start.6 = (f32[64,64]{1,0:T(8,128)}, f32[64,64]{1,0:T(8,128)}, u32[]{:S(2)}, u32[]{:S(2)}) collective-permute-start(f32[64,64]{1,0:T(8,128)} %get-tuple-element.8), channel_id=1, source_target_pairs={{0,1},{1,2},{2,3},{3,4},{4,5},{5,6},{6,7},{7,8},{8,9},{9,10},{10,1... | collective-permute-start | bytes 49160 | tf_op jit(solution)/shard_map/ppermute | solution.py:16
  204.0 289.3 %copy-start.5 = (f32[1024,64]{0,1:T(8,128)S(1)}, f32[1024,64]{0,1:T(8,128)}, u32[]{:S(2)}) copy-start(f32[1024,64]{0,1:T(8,128)} %get-tuple-element.15) | copy-start | bytes 786436
  204.0 286.6 %collective-permute-start.5 = (f32[64,64]{1,0:T(8,128)}, f32[64,64]{1,0:T(8,128)}, u32[]{:S(2)}, u32[]{:S(2)}) collective-permute-start(f32[64,64]{1,0:T(8,128)} %get-tuple-element.9), channel_id=1, source_target_pairs={{1,0},{2,1},{3,2},{4,3},{5,4},{6,5},{7,6},{8,7},{9,8},{10,9},{11,1... | collective-permute-start | bytes 49160 | tf_op jit(solution)/shard_map/ppermute | solution.py:16
  207.8 286.6 %copy-start.4 = (bf16[1024,512]{1,0:T(8,128)(2,1)S(1)}, bf16[1024,512]{1,0:T(8,128)(2,1)}, u32[]{:S(2)}) copy-start(bf16[1024,512]{1,0:T(8,128)(2,1)} %param.11) | copy-start | bytes 3145732
  207.8 286.5 %copy-start.8 = (bf16[512,64]{0,1:T(8,128)(2,1)S(1)}, bf16[512,64]{0,1:T(8,128)(2,1)}, u32[]{:S(2)}) copy-start(bf16[512,64]{0,1:T(8,128)(2,1)} %param.13) | copy-start | bytes 196612
Sparse Core Ops, SparseCore 0:
  494.5 266.3 all-reduce.2
where the time goes:
time: 772 us; the launch traced here: 771 us
  blocking collectives  283 us (37%)
  waiting for transfers between devices  269 us (35%)
  other arithmetic  94.3 us (12%)
  local copies, waits for them, and re-layouts  67.9 us (9%)
  starting transfers between devices  26.9 us (3%)
  matrix products  15.2 us (2%)
  between operations  14.3 us (2%)
    psum x1, blocking collectives, per_device(): lax.psum((grad_down, grad_basis, grad_up), 'graph')  283 us
    psum x1, waiting for transfers between devices, per_device(): lax.psum((grad_down, grad_basis, grad_up), 'graph')  265 us
    scatter-add x1, other arithmetic, per_device(): jax.ops.segment_sum(source_grad, triplet_source, num_segments=table.shape...  44.5 us
    scatter-add x1, other arithmetic, per_device(): jax.ops.segment_sum(message, triplet_target, num_segments=edge_count)  44.4 us
    gather x2, local copies, waits for them, and re-layouts, per_device(): source_rows = table[triplet_source]  29.6 us
    ppermute x8, starting transfers between devices, shifted(): lax.ppermute(value, axis, [(source, source + steps) for source in range(i...  26.8 us
    gather x2, local copies, waits for them, and re-layouts, per_device(): gate = valid * target_grad[triplet_target].astype(jnp.float32)  25.7 us
  transfers between devices with their start and end apart: 9, of which 2 were waited for; matrix products, arithmetic and copies ran while one was open for 1% of the time, Pallas kernels for 0%

commit v1 on v0

v1 whole, which is shorter than its diff:
```python
import functools

import jax
import jax.numpy as jnp
from jax import lax
from jax.experimental import pallas as pl
from jax.experimental.pallas import tpu as pltpu
from jax.sharding import PartitionSpec as P

F32 = jnp.float32
BF16 = jnp.bfloat16
I32 = jnp.int32
residual_scale = 0.7071067811865476
neighbour_offsets = (-2, -1, 1, 2)
PEERS = 4
Y = 4
Z = 16
N = Y * Z
E = 1024
D = 512
TRIP = 64
NB = 42
TRIPS = 8192
LO = 256
TILES = TRIPS // 1024
COLS = (((1,), (1,)), ((), ()))


def sigmoid(value):
    return 0.5 * jnp.tanh(0.5 * value) + 0.5


def slope_of(value):
    sigma = sigmoid(value)
    return sigma * (1.0 + value * (1.0 - sigma))


def dot(a, b):
    return jnp.dot(a, b, preferred_element_type=F32)


def dot_cols(a, b):
    return lax.dot_general(a, b, COLS, preferred_element_type=F32)


def stack_groups(wide, groups):
    return jnp.concatenate([wide[:, LO * h : LO * (h + 1)] for h in range(groups)], axis=0)


def unstack_groups(tall, groups):
    return jnp.concatenate([tall[TRIP * h : TRIP * (h + 1), :] for h in range(groups)], axis=1)


def one_hot(iota_ref, row):
    tile = jnp.broadcast_to(row, (16, row.shape[1])).astype(BF16)
    one = jnp.ones(tile.shape, BF16)
    zero = jnp.zeros(tile.shape, BF16)
    return jnp.concatenate(
        [jnp.where(iota_ref[16 * k : 16 * k + 16, :] == tile, one, zero) for k in range(LO // 16)],
        axis=0,
    )


def pick(grouped, row, groups, fallback):
    held = jnp.broadcast_to(row, (TRIP, row.shape[1]))
    value = fallback
    for h in range(groups - 1, -1, -1):
        value = jnp.where(held == float(h), grouped[TRIP * h : TRIP * (h + 1), :], value)
    return value


def spread(value, row, groups):
    held = jnp.broadcast_to(row, value.shape).astype(BF16)
    zero = jnp.zeros(value.shape, BF16)
    return jnp.concatenate(
        [jnp.where(held == jnp.asarray(h, BF16), value, zero) for h in range(groups)], axis=0
    )


def remote(src, dst, send_sem, recv_sem, where):
    return pltpu.make_async_remote_copy(
        src_ref=src,
        dst_ref=dst,
        send_sem=send_sem,
        recv_sem=recv_sem,
        device_id={"graph": where},
        device_id_type=pl.DeviceIdType.MESH,
    )


class Reduction:
    def __init__(self, my, mz, own, sent, got_y, pieces, got_z, done, sems):
        self.my, self.mz = my, mz
        self.own, self.sent, self.got_y = own, sent, got_y
        self.pieces, self.got_z, self.done = pieces, got_z, done
        self.sy, self.ry, self.sz, self.rz, self.sgz, self.rgz, self.sgy, self.rgy = sems
        self.basis = sent.shape[2] > D

    def y_peer(self, step):
        row = lax.rem(self.my + step, Y)
        return row, self.mz * Y + row

    def z_peer(self, step):
        col = lax.rem(self.mz + step, Z)
        return col, col * Y + self.my

    def y_copy(self, step):
        row, where = self.y_peer(step)
        return remote(
            self.sent.at[row], self.got_y.at[step - 1], self.sy.at[step - 1], self.ry.at[step - 1], where
        )

    def z_copy(self, step):
        col, where = self.z_peer(step)
        return remote(
            self.pieces.at[col], self.got_z.at[step - 1], self.sz.at[step - 1], self.rz.at[step - 1], where
        )

    def gz_copy(self, step):
        _, where = self.z_peer(step)
        block = self.done.at[self.my, self.mz]
        return remote(block, block, self.sgz.at[step - 1], self.rgz.at[step - 1], where)

    def gy_copy(self, step):
        _, where = self.y_peer(step)
        block = self.done.at[self.my]
        return remote(block, block, self.sgy.at[step - 1], self.rgy.at[step - 1], where)

    def start(self):
        for step in range(1, Y):
            self.y_copy(step).start()

    def second(self):
        for step in range(1, Y):
            self.y_copy(step).wait_recv()
        total = self.own[self.my]
        for step in range(Y - 1):
            total = total + self.got_y[step].astype(F32)
        for z in range(Z):
            a, b = z // 4, z % 4
            self.pieces[z, 0:4, :] = total[4 * a : 4 * a + 4, 128 * b : 128 * b + 128].astype(BF16)
            if self.basis:
                self.pieces[z, 4:8, :] = jnp.broadcast_to(
                    total[z : z + 1, D : D + 128], (4, 128)
                ).astype(BF16)
        for step in range(1, Z):
            self.z_copy(step).start()

    def third(self):
        for step in range(1, Z):
            self.z_copy(step).wait_recv()
        total = self.pieces[self.mz].astype(F32)
        for step in range(Z - 1):
            total = total + self.got_z[step].astype(F32)
        self.done[self.my, self.mz] = total.astype(BF16)
        for step in range(1, Z):
            self.gz_copy(step).start()

    def fourth(self):
        for step in range(1, Z):
            self.gz_copy(step).wait_recv()
        for step in range(1, Y):
            self.gy_copy(step).start()

    def finish(self):
        for step in range(1, Y):
            self.gy_copy(step).wait_recv()

    def drain(self):
        for step in range(1, Y):
            self.y_copy(step).wait_send()
            self.gy_copy(step).wait_send()
        for step in range(1, Z):
            self.z_copy(step).wait_send()
            self.gz_copy(step).wait_send()

    def write(self, out_ref):
        for y in range(Y):
            for z in range(Z):
                a, b = z // 4, z % 4
                out_ref[16 * y + 4 * a : 16 * y + 4 * a + 4, 128 * b : 128 * b + 128] = self.done[
                    y, z, 0:4, :
                ].astype(F32)


def kernel(
    edge_hbm,
    cot_hbm,
    bv_hbm,
    down_hbm,
    bw_hbm,
    up_hbm,
    source_hbm,
    target_hbm,
    count_hbm,
    lists_hbm,
    edge_grad_hbm,
    grad_down_ref,
    grad_basis_ref,
    grad_up_ref,
    edge,
    cot,
    bv,
    down,
    bw,
    up,
    source,
    target,
    count,
    lists,
    out,
    iota,
    slo,
    shi,
    tlo,
    thi,
    hot_s,
    hot_t,
    basis,
    rows,
    table,
    acc,
    acc2,
    accb,
    ugrad,
    local_slope,
    fwd_sent,
    fwd_got,
    ret_sent,
    ret_got,
    u_own,
    u_sent,
    u_got_y,
    u_pieces,
    u_got_z,
    u_done,
    d_own,
    d_sent,
    d_got_y,
    d_pieces,
    d_got_z,
    d_done,
    load_sem,
    out_sem,
    fwd_send,
    fwd_recv,
    ret_send,
    ret_recv,
    u_y,
    u_z,
    d_y,
    d_z,
):
    me = lax.axis_index("graph")
    my = lax.rem(me, Y)
    mz = lax.div(me, Y)

    loads = {}
    for at, (name, src, dst) in enumerate(
        (
            ("edge", edge_hbm, edge),
            ("down", down_hbm, down),
            ("lists", lists_hbm, lists),
            ("count", count_hbm, count),
            ("source", source_hbm, source),
            ("target", target_hbm, target),
            ("bw", bw_hbm, bw),
            ("bv", bv_hbm, bv),
            ("up", up_hbm, up),
            ("cot", cot_hbm, cot),
        )
    ):
        loads[name] = pltpu.make_async_copy(src, dst, load_sem.at[at])
        loads[name].start()

    barrier = pltpu.get_barrier_semaphore()

    def hello(where):
        pl.semaphore_signal(
            barrier, inc=1, device_id={"graph": where}, device_id_type=pl.DeviceIdType.MESH
        )

    for offset in neighbour_offsets:
        hello(lax.rem(me + offset + N, N))
    for step in range(1, Y):
        hello(mz * Y + lax.rem(my + step, Y))
    for step in range(1, Z):
        hello(lax.rem(mz + step, Z) * Y + my)

    up_sums = Reduction(
        my, mz, u_own, u_sent, u_got_y, u_pieces, u_got_z, u_done,
        (u_y.at[0], u_y.at[1], u_z.at[0], u_z.at[1], u_z.at[2], u_z.at[3], u_y.at[2], u_y.at[3]),
    )
    down_sums = Reduction(
        my, mz, d_own, d_sent, d_got_y, d_pieces, d_got_z, d_done,
        (d_y.at[0], d_y.at[1], d_z.at[0], d_z.at[1], d_z.at[2], d_z.at[3], d_y.at[2], d_y.at[3]),
    )

    def fwd_copy(k):
        where = lax.rem(me - neighbour_offsets[k] + N, N)
        return remote(fwd_sent.at[k // 2], fwd_got.at[k], fwd_send.at[k], fwd_recv.at[k], where)

    def ret_copy(k):
        where = lax.rem(me + neighbour_offsets[k] + N, N)
        return remote(ret_sent.at[k // 2], ret_got.at[k], ret_send.at[k], ret_recv.at[k], where)

    iota[...] = lax.broadcasted_iota(I32, (LO, 128), 0).astype(F32).astype(BF16)
    lane = lax.broadcasted_iota(I32, (TRIP, 128), 1)
    low_half = lane < 64

    loads["lists"].wait()
    listed = lists[...]
    wide = jnp.concatenate([listed & (LO - 1), listed >> 8], axis=0).astype(F32).astype(BF16)
    repeat = (
        (lax.broadcasted_iota(I32, (64, 256), 1) & 63) == lax.broadcasted_iota(I32, (64, 256), 0)
    )
    tiled = dot(wide, jnp.where(repeat, 1.0, 0.0).astype(BF16))
    own_row = (lax.broadcasted_iota(I32, (PEERS, 256), 1) >> 6) == lax.broadcasted_iota(
        I32, (PEERS, 256), 0
    )
    list_lo = jnp.sum(jnp.where(own_row, tiled[0:PEERS], 0.0), axis=0, keepdims=True)
    list_hi = jnp.sum(jnp.where(own_row, tiled[PEERS : 2 * PEERS], 0.0), axis=0, keepdims=True)
    hot_list = jnp.concatenate(
        [one_hot(iota, list_lo[:, 128 * j : 128 * j + 128]) for j in range(2)], axis=1
    )

    loads["down"].wait()
    down_t = down[...].astype(F32).T.astype(BF16)
    loads["edge"].wait()
    projected = dot_cols(down_t, edge[...])
    sigma = sigmoid(projected)
    local_slope[...] = sigma * (1.0 + projected * (1.0 - sigma))
    hidden = (projected * sigma).astype(BF16)
    table[0 : 4 * TRIP, :] = stack_groups(hidden, 4)
    chosen = pick(dot(table[0 : 4 * TRIP, :], hot_list), list_hi, 4, jnp.zeros((TRIP, 256), F32))
    chosen = chosen.astype(BF16)
    fwd_sent[0] = chosen[:, 0:128]
    fwd_sent[1] = chosen[:, 128:256]
    pl.semaphore_wait(barrier, PEERS + Y - 1 + Z - 1)
    for k in range(PEERS):
        fwd_copy(k).start()

    loads["count"].wait()
    shape = (64, 128)
    at_row, at_lane = lax.broadcasted_iota(I32, shape, 0), lax.broadcasted_iota(I32, shape, 1)
    counts = jnp.broadcast_to(count[...].astype(F32), shape)
    counts = jnp.where((at_lane >> 1) == at_row, counts, 0.0).astype(BF16)
    square = (128, 128)
    halves = (lax.broadcasted_iota(I32, square, 0) & 1) == (lax.broadcasted_iota(I32, square, 1) >> 6)
    counts = dot(counts, jnp.where(halves, 1.0, 0.0).astype(BF16))
    valid = (at_lane & 63).astype(F32) < counts
    loads["source"].wait()
    slo[...] = (source[...] & (LO - 1)).astype(F32)
    shi[...] = (source[...] >> 8).astype(F32)
    loads["target"].wait()
    tlo[...] = (target[...] & (LO - 1)).astype(F32)
    thi[...] = jnp.where(valid, (target[...] >> 8).astype(F32), 8.0)

    loads["bw"].wait()
    bw_t = bw[...].astype(F32).T.astype(BF16)
    loads["bv"].wait()

    def prepare(i, carry):
        tile = pl.ds(pl.multiple_of(i * 8, 8), 8)
        lanes = pl.ds(pl.multiple_of(i * 1024, 1024), 1024)
        s, t = slo[tile, :], tlo[tile, :]
        hot_s[:, lanes] = jnp.concatenate([one_hot(iota, s[q : q + 1]) for q in range(8)], axis=1)
        hot_t[:, lanes] = jnp.concatenate([one_hot(iota, t[q : q + 1]) for q in range(8)], axis=1)
        basis[:, lanes] = dot(bw_t, bv[:, lanes])
        return carry

    lax.fori_loop(0, TILES, prepare, 0)

    def inside(position):
        return (position >= 0) & (position < N)

    for k in range(PEERS):
        fwd_copy(k).wait_recv()
    for j in range(2):
        even = jnp.where(inside(me + neighbour_offsets[2 * j] + 0 * lane), fwd_got[2 * j].astype(F32), 0.0)
        odd = jnp.where(
            inside(me + neighbour_offsets[2 * j + 1] + 0 * lane), fwd_got[2 * j + 1].astype(F32), 0.0
        )
        table[4 * TRIP : 5 * TRIP, 128 * j : 128 * j + 128] = jnp.where(low_half, even, odd).astype(BF16)

    acc[...] = jnp.zeros_like(acc)

    def forward(i, carry):
        tile = pl.ds(pl.multiple_of(i * 8, 8), 8)
        lanes = pl.ds(pl.multiple_of(i * 1024, 1024), 1024)
        s, t = shi[tile, :], thi[tile, :]
        grouped = dot(table[...], hot_s[:, lanes])
        weight = basis[:, lanes]
        found, messages = [], []
        for q in range(8):
            at = slice(128 * q, 128 * q + 128)
            row = pick(grouped[:, at], s[q : q + 1], 4, grouped[4 * TRIP : 5 * TRIP, at])
            found.append(row.astype(BF16))
            messages.append(spread((row * weight[:, at]).astype(BF16), t[q : q + 1], 4))
        rows[:, lanes] = jnp.concatenate(found, axis=1)
        acc[...] += dot_cols(jnp.concatenate(messages, axis=1), hot_t[:, lanes])
        return carry

    lax.fori_loop(0, TILES, forward, 0)

    agg_t = unstack_groups(acc[...], 4)
    agg = agg_t.T.astype(BF16)
    agg_t = agg_t.astype(BF16)
    loads["up"].wait()
    loads["cot"].wait()
    up_w = up[...]
    for b in range(4):
        at = slice(256 * b, 256 * b + 256)
        slope = slope_of(dot(agg[at, :], up_w))
        ugrad[at, :] = (cot[at, :].astype(F32) * residual_scale * slope).astype(BF16)
    table[0 : 4 * TRIP, :] = stack_groups(dot_cols(up_w, ugrad[...]).astype(BF16), 4)
    grad_up = dot(agg_t, ugrad[...])
    for y in range(Y):
        u_own[y] = grad_up[16 * y : 16 * y + 16, :]
        u_sent[y] = grad_up[16 * y : 16 * y + 16, :].astype(BF16)
    up_sums.start()

    acc2[...] = jnp.zeros_like(acc2)
    accb[...] = jnp.zeros_like(accb)

    def backward(i, carry):
        tile = pl.ds(pl.multiple_of(i * 8, 8), 8)
        lanes = pl.ds(pl.multiple_of(i * 1024, 1024), 1024)
        s, t = shi[tile, :], thi[tile, :]
        grouped = dot(table[0 : 4 * TRIP, :], hot_t[:, lanes])
        weight = basis[:, lanes]
        row = rows[:, lanes].astype(F32)
        zero = jnp.zeros((TRIP, 128), F32)
        sources, weights = [], []
        for q in range(8):
            at = slice(128 * q, 128 * q + 128)
            gate = pick(grouped[:, at], t[q : q + 1], 4, zero)
            weights.append((gate * row[:, at]).astype(BF16))
            sources.append(spread((gate * weight[:, at]).astype(BF16), s[q : q + 1], 5))
        acc2[...] += dot_cols(jnp.concatenate(sources, axis=1), hot_s[:, lanes])
        accb[0:NB, 0:TRIP] += dot_cols(bv[:, lanes], jnp.concatenate(weights, axis=1))
        return carry

    lax.fori_loop(0, TILES // 2, backward, 0)
    up_sums.second()
    lax.fori_loop(TILES // 2, TILES, backward, 0)

    for j in range(2):
        ret_sent[j] = acc2[4 * TRIP : 5 * TRIP, 128 * j : 128 * j + 128].astype(BF16)
    for k in range(PEERS):
        ret_copy(k).start()
    up_sums.third()
    for k in range(PEERS):
        ret_copy(k).wait_recv()
    back = []
    for j in range(2):
        even = jnp.where(inside(me - neighbour_offsets[2 * j] + 0 * lane), ret_got[2 * j].astype(F32), 0.0)
        odd = jnp.where(
            inside(me - neighbour_offsets[2 * j + 1] + 0 * lane), ret_got[2 * j + 1].astype(F32), 0.0
        )
        back.append(jnp.where(low_half, even, odd).astype(BF16))
    back = spread(jnp.concatenate(back, axis=1), list_hi, 4)
    hidden_grad = unstack_groups(acc2[0 : 4 * TRIP, :] + dot_cols(back, hot_list), 4)
    gate_t = hidden_grad * local_slope[...]
    gate = gate_t.T.astype(BF16)
    grad_down = dot(gate_t.astype(BF16), edge[...])
    for y in range(Y):
        d_own[y, :, 0:D] = grad_down[16 * y : 16 * y + 16, :]
        d_sent[y, :, 0:D] = grad_down[16 * y : 16 * y + 16, :].astype(BF16)
        padded = accb[16 * y : 16 * y + 16, :] if y < 3 else jnp.zeros((16, 128), F32)
        d_own[y, :, D : D + 128] = padded
        d_sent[y, :, D : D + 128] = padded.astype(BF16)
    down_sums.start()
    up_sums.fourth()

    stores = []
    for b in range(4):
        at = slice(256 * b, 256 * b + 256)
        through = dot(gate[at, :], down_t)
        out[at, :] = (cot[at, :].astype(F32) * residual_scale + through).astype(BF16)
        stores.append(pltpu.make_async_copy(out.at[at], edge_grad_hbm.at[at], out_sem.at[b]))
        stores[b].start()
    down_sums.second()
    up_sums.finish()
    up_sums.write(grad_up_ref)
    down_sums.third()
    for k in range(PEERS):
        fwd_copy(k).wait_send()
        ret_copy(k).wait_send()
    up_sums.drain()
    for store in stores:
        store.wait()
    down_sums.fourth()
    down_sums.finish()
    down_sums.write(grad_down_ref)
    grad_basis = []
    for y in range(3):
        for z in range(Z):
            if 16 * y + z < NB:
                grad_basis_ref[16 * y + z : 16 * y + z + 1, :] = d_done[y, z, 4:5, 0:TRIP].astype(F32)
    down_sums.drain()


def per_device(
    edge_state,
    cotangent,
    basis_values,
    down_weight,
    basis_weight,
    up_weight,
    triplet_source,
    triplet_target,
    block_valid,
    send_lists,
):
    any_space = pl.BlockSpec(memory_space=pl.ANY)
    vmem = pl.BlockSpec(memory_space=pltpu.VMEM)
    dma = pltpu.SemaphoreType.DMA
    edge_grad, grad_down, grad_basis, grad_up = pl.pallas_call(
        kernel,
        out_shape=(
            jax.ShapeDtypeStruct((E, D), BF16),
            jax.ShapeDtypeStruct((TRIP, D), F32),
            jax.ShapeDtypeStruct((NB, TRIP), F32),
            jax.ShapeDtypeStruct((TRIP, D), F32),
        ),
        in_specs=[any_space] * 10,
        out_specs=(any_space, vmem, vmem, vmem),
        scratch_shapes=[
            pltpu.VMEM((E, D), BF16),
            pltpu.VMEM((E, D), BF16),
            pltpu.VMEM((NB, TRIPS), BF16),
            pltpu.VMEM((D, TRIP), BF16),
            pltpu.VMEM((NB, TRIP), BF16),
            pltpu.VMEM((TRIP, D), BF16),
            pltpu.VMEM((64, 128), I32),
            pltpu.VMEM((64, 128), I32),
            pltpu.VMEM((1, 128), I32),
            pltpu.VMEM((PEERS, 64), I32),
            pltpu.VMEM((E, D), BF16),
            pltpu.VMEM((LO, 128), BF16),
            pltpu.VMEM((64, 128), F32),
            pltpu.VMEM((64, 128), F32),
            pltpu.VMEM((64, 128), F32),
            pltpu.VMEM((64, 128), F32),
            pltpu.VMEM((LO, TRIPS), BF16),
            pltpu.VMEM((LO, TRIPS), BF16),
            pltpu.VMEM((TRIP, TRIPS), F32),
            pltpu.VMEM((TRIP, TRIPS), BF16),
            pltpu.VMEM((5 * TRIP, LO), BF16),
            pltpu.VMEM((4 * TRIP, LO), F32),
            pltpu.VMEM((5 * TRIP, LO), F32),
            pltpu.VMEM((48, 128), F32),
            pltpu.VMEM((E, D), BF16),
            pltpu.VMEM((TRIP, E), F32),
            pltpu.VMEM((2, TRIP, 128), BF16),
            pltpu.VMEM((PEERS, TRIP, 128), BF16),
            pltpu.VMEM((2, TRIP, 128), BF16),
            pltpu.VMEM((PEERS, TRIP, 128), BF16),
            pltpu.VMEM((Y, 16, D), F32),
            pltpu.VMEM((Y, 16, D), BF16),
            pltpu.VMEM((Y - 1, 16, D), BF16),
            pltpu.VMEM((Z, 4, 128), BF16),
            pltpu.VMEM((Z - 1, 4, 128), BF16),
            pltpu.VMEM((Y, Z, 4, 128), BF16),
            pltpu.VMEM((Y, 16, D + 128), F32),
            pltpu.VMEM((Y, 16, D + 128), BF16),
            pltpu.VMEM((Y - 1, 16, D + 128), BF16),
            pltpu.VMEM((Z, 8, 128), BF16),
            pltpu.VMEM((Z - 1, 8, 128), BF16),
            pltpu.VMEM((Y, Z, 8, 128), BF16),
            dma((10,)),
            dma((4,)),
            dma((PEERS,)),
            dma((PEERS,)),
            dma((PEERS,)),
            dma((PEERS,)),
            dma((4, Y - 1)),
            dma((4, Z - 1)),
            dma((4, Y - 1)),
            dma((4, Z - 1)),
        ],
        compiler_params=pltpu.CompilerParams(
            collective_id=0, has_side_effects=True, vmem_limit_bytes=48 * 1024 * 1024
        ),
    )(
        edge_state,
        cotangent,
        basis_values,
        down_weight,
        basis_weight,
        up_weight,
        triplet_source.reshape(64, 128),
        triplet_target.reshape(64, 128),
        block_valid.reshape(1, 128),
        send_lists,
    )
    return edge_grad, grad_down.T, grad_basis, grad_up


def solution(mesh):
    return jax.shard_map(
        per_device,
        mesh=mesh,
        in_specs=(
            P(("dp", "graph"), None),
            P(("dp", "graph"), None),
            P(None, ("dp", "graph")),
            P(),
            P(),
            P(),
            P(("dp", "graph")),
            P(("dp", "graph")),
            P(("dp", "graph")),
            P(("dp", "graph"), None),
        ),
        out_specs=(P(("dp", "graph"), None), P("dp", None), P("dp", None), P("dp", None)),
        check_vma=False,
    )
```

time: 772 us -> 74.7 us (0.10)
  blocking collectives: 283 us -> 0 us
  waiting for transfers between devices: 269 us -> 0 us
  other arithmetic: 94.3 us -> 0 us
  Pallas kernels: 0 us -> 66.1 us
  local copies, waits for them, and re-layouts: 67.9 us -> 7.5 us
  starting transfers between devices: 26.9 us -> 0 us
  matrix products: 15.2 us -> 0 us
  between operations: 14.3 us -> 0.76 us
    psum x1 -> x0, blocking collectives: 283 us -> none  [per_device(): lax.psum((grad_down, grad_basis, grad_up), 'graph')]
    psum x1 -> x0, waiting for transfers between devices: 265 us -> none  [per_device(): lax.psum((grad_down, grad_basis, grad_up), 'graph')]
    scatter-add x3 -> x0, other arithmetic: 91.3 us -> none  [the longest x1 44.5 us: per_device(): jax.ops.segment_sum(source_grad, triplet_source, num_segments=table.shape...]
    pallas_call x0 -> x1, Pallas kernels: none -> 66.1 us  [per_device(): pl.pallas_call(kernel, out_shape=(jax.ShapeDtypeStruct((E, D), BF16), jax...]
    gather x5 -> x0, local copies, waits for them, and re-layouts: 56.4 us -> none  [the longest x2 29.6 us: per_device(): source_rows = table[triplet_source]]
    ppermute x8 -> x0, starting transfers between devices: 26.8 us -> none  [shifted(): lax.ppermute(value, axis, [(source, source + steps) for source in range(i...]
    dot_general x9 -> x0, matrix products: 15.2 us -> none  [the longest x1 3.3 us: per_device(): lax.dot_general(basis_values, basis_weight, contract_rows, preferred_elem...]
  transfers between devices with their start and end apart: 9 -> 0, of which waited for: 2 -> 0; matrix products, arithmetic and copies ran while one was open for 1% -> 0% of each run, Pallas kernels for 0% -> 0%
where the time goes in v1:
time: 74.7 us; the launch traced here: 74.4 us
  Pallas kernels  66.1 us (88%)
  local copies, waits for them, and re-layouts  7.5 us (10%)
  between operations  0.76 us (1%)
    pallas_call x1, Pallas kernels, per_device(): pl.pallas_call(kernel, out_shape=(jax.ShapeDtypeStruct((E, D), BF16), jax...  66.1 us
    unnamed x23, local copies, waits for them, and re-layouts  7.5 us

profile of v1, /device:TPU:6, one launch (start us, length us, event | category | flops | bytes accessed | tf_op | source)
XLA Modules:
  0.0 74.4 jit_solution(16958144201272361720)
XLA Ops:
  0.6 0.0 copy-start.3
  0.6 0.0 copy-start.4
  0.7 0.0 copy-start.5
  0.7 0.0 copy-start.6
  0.7 0.0 copy-start.7
  0.7 0.0 copy-start.8
  0.7 1.0 %copy.14.down_hbm = bf16[512,64]{1,0:T(8,128)(2,1)S(1)} copy(bf16[512,64]{0,1:T(8,128)(2,1)} %param.13) | data formatting | bytes 131072 | tf_op args[3]
  1.7 0.0 copy-done.3
  1.7 0.0 copy-done.4
  1.7 0.0 copy-done.5
  1.7 0.0 copy-done.6
  1.7 0.0 copy-done.7
  1.8 0.0 copy-done.8
  1.8 0.0 copy-start
  1.8 1.2 %copy-done = bf16[1024,512]{1,0:T(8,128)(2,1)S(1)} copy-done((bf16[1024,512]{1,0:T(8,128)(2,1)S(1)}, bf16[1024,512]{1,0:T(8,128)(2,1)}, u32[]{:S(2)}) %copy-start) | copy-done | bytes 1048600
  3.0 0.0 copy-start.1
  3.0 1.2 %copy-done.1 = bf16[1024,512]{1,0:T(8,128)(2,1)S(1)} copy-done((bf16[1024,512]{1,0:T(8,128)(2,1)S(1)}, bf16[1024,512]{1,0:T(8,128)(2,1)}, u32[]{:S(2)}) %copy-start.1) | copy-done | bytes 1048600
  4.2 0.0 copy-start.2
  4.2 1.1 %copy-done.2 = bf16[42,8192]{1,0:T(8,128)(2,1)S(1)} copy-done((bf16[42,8192]{1,0:T(8,128)(2,1)S(1)}, bf16[42,8192]{1,0:T(8,128)(2,1)}, u32[]{:S(2)}) %copy-start.2) | copy-done | bytes 688152
  5.4 66.1 %shard_map.129 = (bf16[1024,512]{1,0:T(8,128)(2,1)S(1)}, f32[64,512]{1,0:T(8,128)S(1)}, f32[42,64]{1,0:T(8,128)S(1)}, f32[64,512]{1,0:T(8,128)S(1)}) custom-call(bf16[1024,512]{1,0:T(8,128)(2,1)S(1)} %copy-done, bf16[1024,512]{1,0:T(8,128)(2,1)S(1)} %copy-done.1, bf16[42,8192]{1,0:T(8,128)(2,1)S(1)} %copy-done.2, bf16[512,64]{1,0:T(8,128)(2,1)S(1)} %copy.14.down_hbm, ...), custom_call_target="tpu_custom_call" | custom-call | tf_op jit(solution)/shard_map/pallas_call | solution.py:519
  71.5 1.0 %copy.19 = bf16[1024,512]{1,0:T(8,128)(2,1)} copy(bf16[1024,512]{1,0:T(8,128)(2,1)S(1)} %get-tuple-element.16) | data formatting | bytes 2097152
  72.5 0.7 copy.20
  73.1 0.6 copy.21
  73.7 0.7 copy.22
Async XLA Ops:
  0.6 1.1 %copy-start.3 = (bf16[64,512]{1,0:T(8,128)(2,1)S(1)}, bf16[64,512]{1,0:T(8,128)(2,1)}, u32[]{:S(2)}) copy-start(bf16[64,512]{1,0:T(8,128)(2,1)} %up_hbm.1) | copy-start | bytes 196612
  0.6 1.1 %copy-start.4 = (s32[8192]{0:T(1024)S(1)}, s32[8192]{0:T(1024)}, u32[]{:S(2)}) copy-start(s32[8192]{0:T(1024)} %param.16) | copy-start | bytes 98308
  0.7 1.1 %copy-start.5 = (s32[8192]{0:T(1024)S(1)}, s32[8192]{0:T(1024)}, u32[]{:S(2)}) copy-start(s32[8192]{0:T(1024)} %param.17) | copy-start | bytes 98308
  0.7 1.1 %copy-start.6 = (bf16[42,64]{1,0:T(8,128)(2,1)S(1)}, bf16[42,64]{1,0:T(8,128)(2,1)}, u32[]{:S(2)}) copy-start(bf16[42,64]{1,0:T(8,128)(2,1)} %bw_hbm.1) | copy-start | bytes 16132
  0.7 1.1 %copy-start.7 = (s32[4,64]{1,0:T(4,128)S(1)}, s32[4,64]{1,0:T(4,128)}, u32[]{:S(2)}) copy-start(s32[4,64]{1,0:T(4,128)} %lists_hbm.1) | copy-start | bytes 3076
  0.7 1.1 %copy-start.8 = (s32[128]{0:T(128)S(1)}, s32[128]{0:T(128)}, u32[]{:S(2)}) copy-start(s32[128]{0:T(128)} %param.18) | copy-start | bytes 1540
  1.8 1.2 %copy-start = (bf16[1024,512]{1,0:T(8,128)(2,1)S(1)}, bf16[1024,512]{1,0:T(8,128)(2,1)}, u32[]{:S(2)}) copy-start(bf16[1024,512]{1,0:T(8,128)(2,1)} %edge_hbm.1) | copy-start | bytes 3145732
  3.0 1.2 %copy-start.1 = (bf16[1024,512]{1,0:T(8,128)(2,1)S(1)}, bf16[1024,512]{1,0:T(8,128)(2,1)}, u32[]{:S(2)}) copy-start(bf16[1024,512]{1,0:T(8,128)(2,1)} %cot_hbm.1) | copy-start | bytes 3145732
  4.2 1.1 %copy-start.2 = (bf16[42,8192]{1,0:T(8,128)(2,1)S(1)}, bf16[42,8192]{1,0:T(8,128)(2,1)}, u32[]{:S(2)}) copy-start(bf16[42,8192]{1,0:T(8,128)(2,1)} %bv_hbm.1) | copy-start | bytes 2064388

commit v2 on v1

v2 whole, which is shorter than its diff:
```python
import functools

import jax
import jax.numpy as jnp
from jax import lax
from jax.experimental import pallas as pl
from jax.experimental.pallas import tpu as pltpu
from jax.sharding import PartitionSpec as P

F32 = jnp.float32
BF16 = jnp.bfloat16
I32 = jnp.int32
residual_scale = 0.7071067811865476
neighbour_offsets = (-2, -1, 1, 2)
PEERS = 4
N = 64
NEAR = 8
FAR = N // NEAR
SLOT = 64
E = 1024
D = 512
TRIP = 64
NB = 42
TRIPS = 8192
LO = 256
CHUNK = 8192
ROWS = CHUNK // 128
STEPS = TRIPS // CHUNK
COLS = (((1,), (1,)), ((), ()))


def sigmoid(value):
    return 0.5 * jnp.tanh(0.5 * value) + 0.5


def slope_of(value):
    sigma = sigmoid(value)
    return sigma * (1.0 + value * (1.0 - sigma))


def dot(a, b):
    return jnp.dot(a, b, preferred_element_type=F32)


def dot_cols(a, b):
    return lax.dot_general(a, b, COLS, preferred_element_type=F32)


def stack_groups(wide, groups):
    return jnp.concatenate([wide[:, LO * h : LO * (h + 1)] for h in range(groups)], axis=0)


def unstack_groups(tall, groups):
    return jnp.concatenate([tall[TRIP * h : TRIP * (h + 1), :] for h in range(groups)], axis=1)


def one_hot(iota_ref, row):
    tile = jnp.broadcast_to(row, (16, row.shape[1])).astype(BF16)
    one = jnp.ones(tile.shape, BF16)
    zero = jnp.zeros(tile.shape, BF16)
    return jnp.concatenate(
        [jnp.where(iota_ref[16 * k : 16 * k + 16, :] == tile, one, zero) for k in range(LO // 16)],
        axis=0,
    )


def pick(grouped, row, groups, fallback):
    held = jnp.broadcast_to(row, (TRIP, row.shape[1]))
    value = fallback
    for h in range(groups - 1, -1, -1):
        value = jnp.where(held == float(h), grouped[TRIP * h : TRIP * (h + 1), :], value)
    return value


def spread(value, row, groups):
    held = jnp.broadcast_to(row, value.shape).astype(BF16)
    zero = jnp.zeros(value.shape, BF16)
    return jnp.concatenate(
        [jnp.where(held == jnp.asarray(h, BF16), value, zero) for h in range(groups)], axis=0
    )


def remote(src, dst, send_sem, recv_sem, where):
    return pltpu.make_async_remote_copy(
        src_ref=src,
        dst_ref=dst,
        send_sem=send_sem,
        recv_sem=recv_sem,
        device_id={"graph": where},
        device_id_type=pl.DeviceIdType.MESH,
    )


def near_peer(me, step):
    at = lax.rem(lax.rem(me, NEAR) + step, NEAR)
    return at, lax.div(me, NEAR) * NEAR + at


def far_peer(me, step):
    return lax.rem(me + NEAR * step, N)


class Reduction:
    def __init__(self, me, sent, got, far, done, sems):
        self.me, self.chunk, self.group = me, lax.rem(me, NEAR), lax.div(me, NEAR)
        self.sent, self.got, self.far, self.done, self.sems = sent, got, far, done, sems

    def scatter(self, step):
        at, where = near_peer(self.me, step)
        return remote(
            self.sent.at[at],
            self.got.at[step - 1],
            self.sems.at[0, step - 1],
            self.sems.at[1, step - 1],
            where,
        )

    def exchange(self, step):
        block = self.far.at[self.group]
        return remote(
            block,
            block,
            self.sems.at[2, step - 1],
            self.sems.at[3, step - 1],
            far_peer(self.me, step),
        )

    def gather(self, step):
        _, where = near_peer(self.me, step)
        block = self.done.at[self.chunk]
        return remote(
            block, block, self.sems.at[4, step - 1], self.sems.at[5, step - 1], where
        )

    def start(self):
        for step in range(1, NEAR):
            self.scatter(step).start()

    def second(self):
        for step in range(1, NEAR):
            self.scatter(step).wait_recv()
        total = self.sent[self.chunk].astype(F32)
        for step in range(NEAR - 1):
            total = total + self.got[step].astype(F32)
        self.far[self.group] = total.astype(BF16)
        for step in range(1, FAR):
            self.exchange(step).start()

    def third(self):
        for step in range(1, FAR):
            self.exchange(step).wait_recv()
        total = self.far[0].astype(F32)
        for group in range(1, FAR):
            total = total + self.far[group].astype(F32)
        self.done[self.chunk] = total.astype(BF16)
        for step in range(1, NEAR):
            self.gather(step).start()

    def finish(self):
        for step in range(1, NEAR):
            self.gather(step).wait_recv()

    def drain_early(self):
        for step in range(1, NEAR):
            self.scatter(step).wait_send()
        for step in range(1, FAR):
            self.exchange(step).wait_send()

    def drain(self):
        for step in range(1, NEAR):
            self.gather(step).wait_send()


def chunk_place(at):
    row, lane = 16 * (at // 2), 256 * (at % 2)
    return slice(row, row + 16), slice(lane, lane + 256)


def kernel(
    edge_hbm,
    cot_hbm,
    bv_hbm,
    down_hbm,
    bw_hbm,
    up_hbm,
    source_hbm,
    target_hbm,
    count_hbm,
    lists_hbm,
    edge_grad_ref,
    grad_down_ref,
    grad_basis_ref,
    grad_up_ref,
    edge,
    cot,
    bv,
    down,
    bw,
    up,
    source,
    target,
    count,
    lists,
    iota,
    slo,
    shi,
    tlo,
    thi,
    hot_list,
    hot_s,
    hot_t,
    basis,
    rows,
    table,
    acc,
    acc2,
    accb,
    ugrad,
    local_slope,
    fwd_sent,
    fwd_got,
    state_sent,
    state_got,
    ret_sent,
    ret_got,
    u_sent,
    u_got,
    u_far,
    u_done,
    d_sent,
    d_got,
    d_far,
    d_done,
    load_sem,
    fwd_sem,
    state_sem,
    ret_sem,
    u_sem,
    d_sem,
):
    me = lax.axis_index("graph")
    barrier = pltpu.get_barrier_semaphore()

    def hello(where):
        pl.semaphore_signal(
            barrier, inc=1, device_id={"graph": where}, device_id_type=pl.DeviceIdType.MESH
        )

    loads = {}
    for at, (name, src, dst) in enumerate(
        (
            ("lists", lists_hbm, lists),
            ("edge", edge_hbm, edge),
            ("down", down_hbm, down),
            ("count", count_hbm, count),
            ("source", source_hbm, source),
            ("target", target_hbm, target),
            ("bw", bw_hbm, bw),
            ("bv", bv_hbm, bv),
            ("up", up_hbm, up),
            ("cot", cot_hbm, cot),
        )
    ):
        loads[name] = pltpu.make_async_copy(src, dst, load_sem.at[at])
        loads[name].start()

    for step in range(1, FAR):
        hello(far_peer(me, step))
    for step in range(1, NEAR):
        hello(near_peer(me, step)[1])
    for offset in neighbour_offsets:
        hello(lax.rem(me + offset + N, N))

    up_sums = Reduction(me, u_sent, u_got, u_far, u_done, u_sem)
    down_sums = Reduction(me, d_sent, d_got, d_far, d_done, d_sem)

    def owner_of(k):
        return lax.rem(me + neighbour_offsets[k] + N, N)

    def reader_of(k):
        return lax.rem(me - neighbour_offsets[k] + N, N)

    def fwd_copy(k):
        return remote(
            fwd_sent.at[k // 2], fwd_got.at[k], fwd_sem.at[0, k], fwd_sem.at[1, k], reader_of(k)
        )

    def state_copy(k):
        return remote(
            state_sent.at[k], state_got.at[k], state_sem.at[0, k], state_sem.at[1, k], reader_of(k)
        )

    def ret_copy(k):
        return remote(
            ret_sent.at[k // 2], ret_got.at[k], ret_sem.at[0, k], ret_sem.at[1, k], owner_of(k)
        )

    iota[...] = lax.broadcasted_iota(I32, (LO, 128), 0).astype(F32).astype(BF16)
    slot_lane = lax.broadcasted_iota(I32, (TRIP, LO), 1)
    slot_offset = jnp.where(
        slot_lane < 2 * SLOT,
        jnp.where(slot_lane < SLOT, neighbour_offsets[0], neighbour_offsets[1]),
        jnp.where(slot_lane < 3 * SLOT, neighbour_offsets[2], neighbour_offsets[3]),
    )
    even_slot = (slot_lane & SLOT) == 0
    named = (me + slot_offset >= 0) & (me + slot_offset < N)
    read = (me - slot_offset >= 0) & (me - slot_offset < N)

    def joined(got):
        even = jnp.concatenate([got[0].astype(F32), got[2].astype(F32)], axis=1)
        odd = jnp.concatenate([got[1].astype(F32), got[3].astype(F32)], axis=1)
        return jnp.where(even_slot, even, odd)

    loads["lists"].wait()
    listed = lists[...]
    shape = (PEERS * SLOT, PEERS)
    pick_list = (lax.broadcasted_iota(I32, shape, 0) >> 6) == lax.broadcasted_iota(I32, shape, 1)
    pick_list = jnp.where(pick_list, 1.0, 0.0).astype(BF16)
    shape = (PEERS * SLOT, SLOT)
    own = (lax.broadcasted_iota(I32, shape, 0) & (SLOT - 1)) == lax.broadcasted_iota(I32, shape, 1)
    high = dot(pick_list, (listed >> 8).astype(F32).astype(BF16))
    low = dot(pick_list, (listed & (LO - 1)).astype(F32).astype(BF16))
    number = jnp.sum(jnp.where(own, high * LO + low, 0.0), axis=1, keepdims=True)
    lanes = lax.broadcasted_iota(I32, (1, 128), 1).astype(F32)
    for b in range(E // 128):
        hot_list[:, 128 * b : 128 * b + 128] = jnp.where(
            lanes + float(128 * b) == number, 1.0, 0.0
        ).astype(BF16)

    loads["down"].wait()
    loads["edge"].wait()
    projected = dot_cols(down[...], edge[...])
    sigma = sigmoid(projected)
    local_slope[...] = sigma * (1.0 + projected * (1.0 - sigma))
    hidden = (projected * sigma).astype(BF16)
    chosen = dot_cols(hidden, hot_list[...]).astype(BF16)
    fwd_sent[0] = chosen[:, 0:128]
    fwd_sent[1] = chosen[:, 128:256]
    table[0 : 4 * TRIP, :] = stack_groups(hidden, 4)
    pl.semaphore_wait(barrier, PEERS + NEAR - 1 + FAR - 1)
    for k in range(PEERS):
        fwd_copy(k).start()
    for k in range(PEERS):
        state_sent[k] = dot(hot_list[SLOT * k : SLOT * (k + 1), :], edge[...]).astype(BF16)
    for k in range(PEERS):
        state_copy(k).start()

    loads["count"].wait()
    shape = (64, 128)
    at_row, at_lane = lax.broadcasted_iota(I32, shape, 0), lax.broadcasted_iota(I32, shape, 1)
    counts = jnp.broadcast_to(count[...].astype(F32), shape)
    counts = jnp.where((at_lane >> 1) == at_row, counts, 0.0).astype(BF16)
    square = (128, 128)
    halves = (lax.broadcasted_iota(I32, square, 0) & 1) == (lax.broadcasted_iota(I32, square, 1) >> 6)
    counts = dot(counts, jnp.where(halves, 1.0, 0.0).astype(BF16))
    valid = (at_lane & 63).astype(F32) < counts
    loads["source"].wait()
    slo[...] = (source[...] & (LO - 1)).astype(F32)
    shi[...] = (source[...] >> 8).astype(F32)
    loads["target"].wait()
    tlo[...] = (target[...] & (LO - 1)).astype(F32)
    thi[...] = jnp.where(valid, (target[...] >> 8).astype(F32), 8.0)

    loads["bw"].wait()
    bw_t = bw[...].astype(F32).T.astype(BF16)
    loads["bv"].wait()

    def place(i):
        lanes = pl.ds(pl.multiple_of(i * CHUNK, CHUNK), CHUNK)
        return lanes, [pl.ds(i * ROWS + q, 1) for q in range(ROWS)]

    def prepare(i, carry):
        lanes, at = place(i)
        hot = jnp.concatenate([one_hot(iota, slo[a, :]) for a in at], axis=1)
        hot_s[:, lanes] = hot
        hot_t[:, lanes] = jnp.concatenate([one_hot(iota, tlo[a, :]) for a in at], axis=1)
        basis[:, lanes] = dot(bw_t, bv[:, lanes])
        grouped = dot(table[0 : 4 * TRIP, :], hot)
        found = []
        for q in range(ROWS):
            part = grouped[:, 128 * q : 128 * q + 128]
            found.append(pick(part, shi[at[q], :], 3, part[3 * TRIP : 4 * TRIP, :]).astype(BF16))
        rows[:, lanes] = jnp.concatenate(found, axis=1)
        return carry

    lax.fori_loop(0, STEPS, prepare, 0)

    for k in range(PEERS):
        fwd_copy(k).wait_recv()
    table[4 * TRIP : 5 * TRIP, :] = jnp.where(named, joined(fwd_got), 0.0).astype(BF16)
    acc[...] = jnp.zeros_like(acc)

    def forward(i, carry):
        lanes, at = place(i)
        arrived = dot(table[4 * TRIP : 5 * TRIP, :], hot_s[:, lanes])
        weight = basis[:, lanes]
        near_rows = rows[:, lanes].astype(F32)
        found, messages = [], []
        for q in range(ROWS):
            part = slice(128 * q, 128 * q + 128)
            held = jnp.broadcast_to(shi[at[q], :], (TRIP, 128))
            row = jnp.where(held == 4.0, arrived[:, part], near_rows[:, part])
            found.append(row.astype(BF16))
            messages.append(spread((row * weight[:, part]).astype(BF16), thi[at[q], :], 4))
        rows[:, lanes] = jnp.concatenate(found, axis=1)
        acc[...] += dot_cols(jnp.concatenate(messages, axis=1), hot_t[:, lanes])
        return carry

    lax.fori_loop(0, STEPS, forward, 0)

    agg_t = unstack_groups(acc[...], 4)
    agg = agg_t.T.astype(BF16)
    agg_t = agg_t.astype(BF16)
    loads["up"].wait()
    loads["cot"].wait()
    up_w = up[...]
    for b in range(4):
        at = slice(256 * b, 256 * b + 256)
        slope = slope_of(dot(agg[at, :], up_w))
        ugrad[at, :] = (cot[at, :].astype(F32) * residual_scale * slope).astype(BF16)
    table[0 : 4 * TRIP, :] = stack_groups(dot_cols(up_w, ugrad[...]).astype(BF16), 4)
    grad_up = dot(agg_t, ugrad[...]).astype(BF16)
    for at in range(NEAR):
        u_sent[at] = grad_up[chunk_place(at)]
    up_sums.start()

    acc2[...] = jnp.zeros_like(acc2)
    accb[...] = jnp.zeros_like(accb)

    def backward(i, carry):
        lanes, at = place(i)
        grouped = dot(table[0 : 4 * TRIP, :], hot_t[:, lanes])
        weight = basis[:, lanes]
        row = rows[:, lanes].astype(F32)
        zero = jnp.zeros((TRIP, 128), F32)
        sources, weights = [], []
        for q in range(ROWS):
            part = slice(128 * q, 128 * q + 128)
            gate = pick(grouped[:, part], thi[at[q], :], 4, zero)
            weights.append((gate * row[:, part]).astype(BF16))
            sources.append(spread((gate * weight[:, part]).astype(BF16), shi[at[q], :], 5))
        acc2[...] += dot_cols(jnp.concatenate(sources, axis=1), hot_s[:, lanes])
        accb[0:NB, 0:TRIP] += dot_cols(bv[:, lanes], jnp.concatenate(weights, axis=1))
        return carry

    lax.fori_loop(0, STEPS, backward, 0)

    far_grad = acc2[4 * TRIP : 5 * TRIP, :]
    ret_sent[0] = far_grad[:, 0:128].astype(BF16)
    ret_sent[1] = far_grad[:, 128:256].astype(BF16)
    for k in range(PEERS):
        ret_copy(k).start()
    for k in range(PEERS):
        state_copy(k).wait_recv()
    state = jnp.concatenate([state_got[k] for k in range(PEERS)], axis=0)
    far_gate = far_grad * slope_of(dot_cols(down[...], state))
    far_gate = jnp.where(named, far_gate, 0.0).astype(BF16)
    own_grad = unstack_groups(acc2[0 : 4 * TRIP, :], 4)
    own_gate = (own_grad * local_slope[...]).astype(BF16)
    grad_down = (dot(own_gate, edge[...]) + dot(far_gate, state)).astype(BF16)
    for at in range(NEAR):
        d_sent[at, :, 0:256] = grad_down[chunk_place(at)]
        rest = accb[16 * at : 16 * at + 16, :] if at < 3 else jnp.zeros((16, 128), F32)
        d_sent[at, :, 256:384] = rest.astype(BF16)
    down_sums.start()
    up_sums.second()
    down_sums.second()

    for k in range(PEERS):
        ret_copy(k).wait_recv()
    back = jnp.where(read, joined(ret_got), 0.0).astype(BF16)
    hidden_grad = own_grad + dot(back, hot_list[...])
    gate = (hidden_grad * local_slope[...]).T.astype(BF16)
    for b in range(4):
        at = slice(256 * b, 256 * b + 256)
        through = dot(gate[at, :], down[...])
        edge_grad_ref[at, :] = (cot[at, :].astype(F32) * residual_scale + through).astype(BF16)
    up_sums.third()
    for k in range(PEERS):
        fwd_copy(k).wait_send()
        state_copy(k).wait_send()
        ret_copy(k).wait_send()
    up_sums.drain_early()
    down_sums.third()
    up_sums.finish()
    for at in range(NEAR):
        grad_up_ref[chunk_place(at)] = u_done[at].astype(F32)
    up_sums.drain()
    down_sums.drain_early()
    down_sums.finish()
    for at in range(NEAR):
        grad_down_ref[chunk_place(at)] = d_done[at, :, 0:256].astype(F32)
    for at in range(3):
        count_rows = min(16, NB - 16 * at)
        grad_basis_ref[16 * at : 16 * at + count_rows, :] = d_done[
            at, 0:count_rows, 256 : 256 + TRIP
        ].astype(F32)
    down_sums.drain()


def store_kernel(a, b, c, d, a_hbm, b_hbm, c_hbm, d_hbm, sem):
    copies = [
        pltpu.make_async_copy(src, dst, sem.at[at])
        for at, (src, dst) in enumerate(((a, a_hbm), (b, b_hbm), (c, c_hbm), (d, d_hbm)))
    ]
    for copy in copies:
        copy.start()
    for copy in copies:
        copy.wait()


def per_device(
    edge_state,
    cotangent,
    basis_values,
    down_weight,
    basis_weight,
    up_weight,
    triplet_source,
    triplet_target,
    block_valid,
    send_lists,
):
    hbm = pl.BlockSpec(memory_space=pltpu.HBM)
    vmem = pl.BlockSpec(memory_space=pltpu.VMEM)
    dma = pltpu.SemaphoreType.DMA
    out_shape = (
        jax.ShapeDtypeStruct((E, D), BF16),
        jax.ShapeDtypeStruct((TRIP, D), F32),
        jax.ShapeDtypeStruct((NB, TRIP), F32),
        jax.ShapeDtypeStruct((TRIP, D), F32),
    )
    args = (
        edge_state,
        cotangent,
        basis_values,
        down_weight.T,
        basis_weight,
        up_weight,
        triplet_source.reshape(64, 128),
        triplet_target.reshape(64, 128),
        block_valid.reshape(1, 128),
        send_lists,
    )
    args = [pltpu.with_memory_space_constraint(arg, pltpu.HBM) for arg in args]
    results = pl.pallas_call(
        kernel,
        out_shape=out_shape,
        in_specs=[hbm] * 10,
        out_specs=(vmem,) * 4,
        scratch_shapes=[
            pltpu.VMEM((E, D), BF16),
            pltpu.VMEM((E, D), BF16),
            pltpu.VMEM((NB, TRIPS), BF16),
            pltpu.VMEM((TRIP, D), BF16),
            pltpu.VMEM((NB, TRIP), BF16),
            pltpu.VMEM((TRIP, D), BF16),
            pltpu.VMEM((64, 128), I32),
            pltpu.VMEM((64, 128), I32),
            pltpu.VMEM((1, 128), I32),
            pltpu.VMEM((PEERS, SLOT), I32),
            pltpu.VMEM((LO, 128), BF16),
            pltpu.VMEM((64, 128), F32),
            pltpu.VMEM((64, 128), F32),
            pltpu.VMEM((64, 128), F32),
            pltpu.VMEM((64, 128), F32),
            pltpu.VMEM((PEERS * SLOT, E), BF16),
            pltpu.VMEM((LO, TRIPS), BF16),
            pltpu.VMEM((LO, TRIPS), BF16),
            pltpu.VMEM((TRIP, TRIPS), F32),
            pltpu.VMEM((TRIP, TRIPS), BF16),
            pltpu.VMEM((5 * TRIP, LO), BF16),
            pltpu.VMEM((4 * TRIP, LO), F32),
            pltpu.VMEM((5 * TRIP, LO), F32),
            pltpu.VMEM((48, 128), F32),
            pltpu.VMEM((E, D), BF16),
            pltpu.VMEM((TRIP, E), F32),
            pltpu.VMEM((2, TRIP, 128), BF16),
            pltpu.VMEM((PEERS, TRIP, 128), BF16),
            pltpu.VMEM((PEERS, SLOT, D), BF16),
            pltpu.VMEM((PEERS, SLOT, D), BF16),
            pltpu.VMEM((2, TRIP, 128), BF16),
            pltpu.VMEM((PEERS, TRIP, 128), BF16),
            pltpu.VMEM((NEAR, 16, 256), BF16),
            pltpu.VMEM((NEAR - 1, 16, 256), BF16),
            pltpu.VMEM((FAR, 16, 256), BF16),
            pltpu.VMEM((NEAR, 16, 256), BF16),
            pltpu.VMEM((NEAR, 16, 384), BF16),
            pltpu.VMEM((NEAR - 1, 16, 384), BF16),
            pltpu.VMEM((FAR, 16, 384), BF16),
            pltpu.VMEM((NEAR, 16, 384), BF16),
            dma((10,)),
            dma((2, PEERS)),
            dma((2, PEERS)),
            dma((2, PEERS)),
            dma((6, NEAR - 1)),
            dma((6, NEAR - 1)),
        ],
        compiler_params=pltpu.CompilerParams(
            collective_id=0, has_side_effects=True, vmem_limit_bytes=48 * 1024 * 1024
        ),
    )(*args)
    edge_grad, grad_down, grad_basis, grad_up = pl.pallas_call(
        store_kernel,
        out_shape=out_shape,
        in_specs=[vmem] * 4,
        out_specs=(hbm,) * 4,
        scratch_shapes=[dma((4,))],
        compiler_params=pltpu.CompilerParams(vmem_limit_bytes=1024 * 1024),
    )(*results)
    return edge_grad, grad_down.T, grad_basis, grad_up


def solution(mesh):
    return jax.shard_map(
        per_device,
        mesh=mesh,
        in_specs=(
            P(("dp", "graph"), None),
            P(("dp", "graph"), None),
            P(None, ("dp", "graph")),
            P(),
            P(),
            P(),
            P(("dp", "graph")),
            P(("dp", "graph")),
            P(("dp", "graph")),
            P(("dp", "graph"), None),
        ),
        out_specs=(P(("dp", "graph"), None), P("dp", None), P("dp", None), P("dp", None)),
        check_vma=False,
    )
```

time: 74.7 us -> 49.5 us (0.66)
  Pallas kernels: 66.1 us -> 48.7 us
  local copies, waits for them, and re-layouts: 7.5 us -> 0 us
    pallas_call x1 -> x2, Pallas kernels: 66.1 us -> 48.7 us  [the longest x1 47.6 us: per_device(): pl.pallas_call(kernel, out_shape=out_shape, in_specs=[hbm] * 10, out_spec...]
    unnamed x23 -> x0, local copies, waits for them, and re-layouts: 7.5 us -> none
where the time goes in v2:
time: 49.5 us; the launch traced here: 49.3 us
  Pallas kernels  48.7 us (98%)
  between operations  0.64 us (1%)
    pallas_call x1, Pallas kernels, per_device(): pl.pallas_call(kernel, out_shape=out_shape, in_specs=[hbm] * 10, out_spec...  47.6 us
    pallas_call x1, Pallas kernels, per_device(): pl.pallas_call(store_kernel, out_shape=out_shape, in_specs=[vmem] * 4, ou...  1.09 us

profile of v2, /device:TPU:6, one launch (start us, length us, event | category | flops | bytes accessed | tf_op | source)
XLA Modules:
  0.0 49.3 jit_solution(13705866882892087158)
XLA Ops:
  0.6 47.6 %shard_map.129 = (bf16[1024,512]{1,0:T(8,128)(2,1)S(1)}, f32[64,512]{1,0:T(8,128)S(1)}, f32[42,64]{1,0:T(8,128)S(1)}, f32[64,512]{1,0:T(8,128)S(1)}) custom-call(bf16[1024,512]{1,0:T(8,128)(2,1)} %edge_hbm.1, bf16[1024,512]{1,0:T(8,128)(2,1)} %cot_hbm.1, bf16[42,8192]{1,0:T(8,128)(2,1)} %bv_hbm.1, bf16[64,512]{1,0:T(8,128)(2,1)} %bitcast.5, ...), custom_call_target="tpu_custom_call" | custom-call | tf_op jit(solution)/shard_map/pallas_call | solution.py:546
  48.2 1.1 %shard_map.130 = (bf16[1024,512]{1,0:T(8,128)(2,1)}, f32[64,512]{1,0:T(8,128)}, f32[42,64]{1,0:T(8,128)}, f32[64,512]{1,0:T(8,128)}) custom-call(bf16[1024,512]{1,0:T(8,128)(2,1)S(1)} %get-tuple-element.12.a, f32[64,512]{1,0:T(8,128)S(1)} %get-tuple-element.13.b, f32[42,64]{1,0:T(8,128)S(1)} %get-tuple-element.14.c, f32[64,512]{1,0:T(8,128)S(1)} %get-tuple-element.15.d), custom_call_target="tpu_custom_call" | custom-call | tf_op jit(solution)/shard_map/pallas_call | solution.py:603

commit v3 on v2

v3 whole, which is shorter than its diff:
```python
import functools

import jax
import jax.numpy as jnp
from jax import lax
from jax.experimental import pallas as pl
from jax.experimental.pallas import tpu as pltpu
from jax.sharding import PartitionSpec as P

F32 = jnp.float32
BF16 = jnp.bfloat16
I32 = jnp.int32
residual_scale = 0.7071067811865476
neighbour_offsets = (-2, -1, 1, 2)
PEERS = 4
N = 64
NEAR = 8
FAR = N // NEAR
SLOT = 64
E = 1024
D = 512
TRIP = 64
NB = 42
TRIPS = 8192
LO = 256
PREPARE_CHUNK = 4096
FORWARD_CHUNK = 4096
BACKWARD_CHUNK = 4096
COLS = (((1,), (1,)), ((), ()))


def sigmoid(value):
    return 0.5 * jnp.tanh(0.5 * value) + 0.5


def slope_of(value):
    half = 0.5 * value
    bent = jnp.tanh(half)
    return (0.5 + 0.5 * bent) * (1.0 + half * (1.0 - bent))


def dot(a, b):
    return jnp.dot(a, b, preferred_element_type=F32)


def dot_cols(a, b):
    return lax.dot_general(a, b, COLS, preferred_element_type=F32)


def stack_groups(wide, groups):
    return jnp.concatenate([wide[:, LO * h : LO * (h + 1)] for h in range(groups)], axis=0)


def unstack_groups(tall, groups):
    return jnp.concatenate([tall[TRIP * h : TRIP * (h + 1), :] for h in range(groups)], axis=1)


def one_hot(iota_ref, row):
    tile = jnp.broadcast_to(row, (16, row.shape[1])).astype(BF16)
    one = jnp.ones(tile.shape, BF16)
    zero = jnp.zeros(tile.shape, BF16)
    return jnp.concatenate(
        [jnp.where(iota_ref[16 * k : 16 * k + 16, :] == tile, one, zero) for k in range(LO // 16)],
        axis=0,
    )


def pick(grouped, row, groups, fallback):
    held = jnp.broadcast_to(row, (TRIP, row.shape[1]))
    value = fallback
    for h in range(groups - 1, -1, -1):
        value = jnp.where(held == float(h), grouped[TRIP * h : TRIP * (h + 1), :], value)
    return value


def spread(value, row, groups):
    held = jnp.broadcast_to(row, value.shape).astype(BF16)
    zero = jnp.zeros(value.shape, BF16)
    return jnp.concatenate(
        [jnp.where(held == jnp.asarray(h, BF16), value, zero) for h in range(groups)], axis=0
    )


def remote(src, dst, send_sem, recv_sem, where):
    return pltpu.make_async_remote_copy(
        src_ref=src,
        dst_ref=dst,
        send_sem=send_sem,
        recv_sem=recv_sem,
        device_id={"graph": where},
        device_id_type=pl.DeviceIdType.MESH,
    )


def near_peer(me, step):
    at = lax.rem(lax.rem(me, NEAR) + step, NEAR)
    return at, lax.div(me, NEAR) * NEAR + at


def far_peer(me, step):
    return lax.rem(me + NEAR * step, N)


NEAR_ORDER = (6, 2, 7, 3, 5, 1, 4)
FAR_ORDER = (4, 3, 5, 2, 6, 1, 7)


class Reduction:
    def __init__(self, me, sent, got, far, done, sems):
        self.me, self.chunk, self.group = me, lax.rem(me, NEAR), lax.div(me, NEAR)
        self.sent, self.got, self.far, self.done, self.sems = sent, got, far, done, sems

    def scatter(self, step):
        at, where = near_peer(self.me, step)
        return remote(
            self.sent.at[at],
            self.got.at[step - 1],
            self.sems.at[0, step - 1],
            self.sems.at[1, step - 1],
            where,
        )

    def exchange(self, step):
        block = self.far.at[self.group]
        return remote(
            block,
            block,
            self.sems.at[2, step - 1],
            self.sems.at[3, step - 1],
            far_peer(self.me, step),
        )

    def gather(self, step):
        _, where = near_peer(self.me, step)
        block = self.done.at[self.chunk]
        return remote(
            block, block, self.sems.at[4, step - 1], self.sems.at[5, step - 1], where
        )

    def start(self):
        for step in NEAR_ORDER:
            self.scatter(step).start()

    def second(self):
        for step in range(1, NEAR):
            self.scatter(step).wait_recv()
        total = self.sent[self.chunk].astype(F32)
        for step in range(NEAR - 1):
            total = total + self.got[step].astype(F32)
        self.far[self.group] = total.astype(BF16)
        for step in FAR_ORDER:
            self.exchange(step).start()

    def third(self):
        for step in range(1, FAR):
            self.exchange(step).wait_recv()
        total = self.far[0].astype(F32)
        for group in range(1, FAR):
            total = total + self.far[group].astype(F32)
        self.done[self.chunk] = total.astype(BF16)
        for step in NEAR_ORDER:
            self.gather(step).start()

    def finish(self):
        for step in range(1, NEAR):
            self.gather(step).wait_recv()

    def drain_early(self):
        for step in range(1, NEAR):
            self.scatter(step).wait_send()
        for step in range(1, FAR):
            self.exchange(step).wait_send()

    def drain(self):
        for step in range(1, NEAR):
            self.gather(step).wait_send()


def chunk_place(at):
    row, lane = 16 * (at // 2), 256 * (at % 2)
    return slice(row, row + 16), slice(lane, lane + 256)


def place(i, size):
    lanes = pl.ds(pl.multiple_of(i * size, size), size)
    return lanes, [pl.ds(i * (size // 128) + q, 1) for q in range(size // 128)]


def greet(where):
    pl.semaphore_signal(
        pltpu.get_barrier_semaphore(),
        inc=1,
        device_id={"graph": where},
        device_id_type=pl.DeviceIdType.MESH,
    )


def start_loads(sem, named):
    loads = {}
    for at, (name, src, dst) in enumerate(named):
        loads[name] = pltpu.make_async_copy(src, dst, sem.at[at])
        loads[name].start()
    return loads


def owner_of(me, k):
    return lax.rem(me + neighbour_offsets[k] + N, N)


def reader_of(me, k):
    return lax.rem(me - neighbour_offsets[k] + N, N)


def slot_offsets():
    slot_lane = lax.broadcasted_iota(I32, (TRIP, LO), 1)
    offset = jnp.where(
        slot_lane < 2 * SLOT,
        jnp.where(slot_lane < SLOT, neighbour_offsets[0], neighbour_offsets[1]),
        jnp.where(slot_lane < 3 * SLOT, neighbour_offsets[2], neighbour_offsets[3]),
    )
    return slot_lane, offset


def gather_kernel(
    edge_hbm,
    bv_hbm,
    down_hbm,
    bw_hbm,
    source_hbm,
    target_hbm,
    count_hbm,
    lists_hbm,
    hot_list,
    hot_s,
    hot_t,
    basis,
    rows,
    table,
    shi,
    thi,
    local_slope,
    far_slope,
    state_got,
    edge,
    bv,
    down,
    bw,
    source,
    target,
    count,
    lists,
    iota,
    slo,
    tlo,
    state_sent,
    load_sem,
    state_sem,
):
    me = lax.axis_index("graph")
    for k in range(PEERS):
        greet(owner_of(me, k))
    loads = start_loads(
        load_sem,
        (
            ("lists", lists_hbm, lists),
            ("edge", edge_hbm, edge),
            ("down", down_hbm, down),
            ("count", count_hbm, count),
            ("source", source_hbm, source),
            ("target", target_hbm, target),
            ("bw", bw_hbm, bw),
            ("bv", bv_hbm, bv),
        ),
    )

    def state_copy(k):
        return remote(
            state_sent.at[k], state_got.at[k], state_sem.at[0, k], state_sem.at[1, k], reader_of(me, k)
        )

    iota[...] = lax.broadcasted_iota(I32, (LO, 128), 0).astype(F32).astype(BF16)

    loads["lists"].wait()
    listed = lists[...]
    shape = (PEERS * SLOT, PEERS)
    pick_list = (lax.broadcasted_iota(I32, shape, 0) >> 6) == lax.broadcasted_iota(I32, shape, 1)
    pick_list = jnp.where(pick_list, 1.0, 0.0).astype(BF16)
    shape = (PEERS * SLOT, SLOT)
    own = (lax.broadcasted_iota(I32, shape, 0) & (SLOT - 1)) == lax.broadcasted_iota(I32, shape, 1)
    high = dot(pick_list, (listed >> 8).astype(F32).astype(BF16))
    low = dot(pick_list, (listed & (LO - 1)).astype(F32).astype(BF16))
    number = jnp.sum(jnp.where(own, high * LO + low, 0.0), axis=1, keepdims=True)
    lanes = lax.broadcasted_iota(I32, (1, 128), 1).astype(F32)
    for b in range(E // 128):
        hot_list[:, 128 * b : 128 * b + 128] = jnp.where(
            lanes + float(128 * b) == number, 1.0, 0.0
        ).astype(BF16)

    loads["edge"].wait()
    listed_rows = dot(hot_list[...], edge[...]).astype(BF16)
    for k in range(PEERS):
        state_sent[k] = listed_rows[SLOT * k : SLOT * (k + 1), :]
    pl.semaphore_wait(pltpu.get_barrier_semaphore(), PEERS)
    for k in (0, 3, 1, 2):
        state_copy(k).start()

    loads["down"].wait()
    projected = dot_cols(down[...], edge[...])
    sigma = sigmoid(projected)
    local_slope[...] = sigma * (1.0 + projected * (1.0 - sigma))
    hidden = (projected * sigma).astype(BF16)
    table[0 : 4 * TRIP, :] = stack_groups(hidden, 4)

    loads["count"].wait()
    shape = (64, 128)
    at_row, at_lane = lax.broadcasted_iota(I32, shape, 0), lax.broadcasted_iota(I32, shape, 1)
    counts = jnp.broadcast_to(count[...].astype(F32), shape)
    counts = jnp.where((at_lane >> 1) == at_row, counts, 0.0).astype(BF16)
    square = (128, 128)
    halves = (lax.broadcasted_iota(I32, square, 0) & 1) == (lax.broadcasted_iota(I32, square, 1) >> 6)
    counts = dot(counts, jnp.where(halves, 1.0, 0.0).astype(BF16))
    valid = (at_lane & 63).astype(F32) < counts
    loads["source"].wait()
    slo[...] = (source[...] & (LO - 1)).astype(F32)
    shi[...] = (source[...] >> 8).astype(F32)
    loads["target"].wait()
    tlo[...] = (target[...] & (LO - 1)).astype(F32)
    thi[...] = jnp.where(valid, (target[...] >> 8).astype(F32), 8.0)

    loads["bw"].wait()
    bw_t = bw[...].astype(F32).T.astype(BF16)
    loads["bv"].wait()

    def prepare(i, carry):
        lanes, at = place(i, PREPARE_CHUNK)
        hot = jnp.concatenate([one_hot(iota, slo[a, :]) for a in at], axis=1)
        hot_s[:, lanes] = hot
        hot_t[:, lanes] = jnp.concatenate([one_hot(iota, tlo[a, :]) for a in at], axis=1)
        basis[:, lanes] = dot(bw_t, bv[:, lanes])
        grouped = dot(table[0 : 4 * TRIP, :], hot)
        found = []
        for q in range(PREPARE_CHUNK // 128):
            part = grouped[:, 128 * q : 128 * q + 128]
            found.append(pick(part, shi[at[q], :], 3, part[3 * TRIP : 4 * TRIP, :]).astype(BF16))
        rows[:, lanes] = jnp.concatenate(found, axis=1)
        return carry

    lax.fori_loop(0, TRIPS // PREPARE_CHUNK, prepare, 0)

    for k in range(PEERS):
        state_copy(k).wait_recv()
    offset = slot_offsets()[1]
    named = (me + offset >= 0) & (me + offset < N)
    state = jnp.concatenate([state_got[k] for k in range(PEERS)], axis=0)
    far_projected = dot_cols(down[...], state)
    sigma = sigmoid(far_projected)
    slope = sigma * (1.0 + far_projected * (1.0 - sigma))
    far_slope[...] = jnp.where(named, slope, 0.0)
    table[4 * TRIP : 5 * TRIP, :] = jnp.where(named, far_projected * sigma, 0.0).astype(BF16)
    for k in range(PEERS):
        state_copy(k).wait_send()


def triplet_kernel(
    edge_hbm,
    cot_hbm,
    bv_hbm,
    down_hbm,
    up_hbm,
    hot_list,
    hot_s,
    hot_t,
    basis,
    rows,
    table,
    shi,
    thi,
    local_slope,
    far_slope,
    state_got,
    edge_grad_ref,
    grad_down_ref,
    grad_basis_ref,
    grad_up_ref,
    edge,
    cot,
    bv,
    down,
    up,
    all_rows,
    target_table,
    acc,
    acc2,
    accb,
    ugrad,
    ret_sent,
    ret_got,
    u_sent,
    u_got,
    u_far,
    u_done,
    d_sent,
    d_got,
    d_far,
    d_done,
    load_sem,
    ret_sem,
    u_sem,
    d_sem,
):
    me = lax.axis_index("graph")
    for step in FAR_ORDER:
        greet(far_peer(me, step))
    for step in NEAR_ORDER:
        greet(near_peer(me, step)[1])
    for k in range(PEERS):
        greet(owner_of(me, k))
    loads = start_loads(
        load_sem,
        (
            ("up", up_hbm, up),
            ("cot", cot_hbm, cot),
            ("bv", bv_hbm, bv),
            ("down", down_hbm, down),
            ("edge", edge_hbm, edge),
        ),
    )
    up_sums = Reduction(me, u_sent, u_got, u_far, u_done, u_sem)
    down_sums = Reduction(me, d_sent, d_got, d_far, d_done, d_sem)

    def ret_copy(k):
        return remote(
            ret_sent.at[k // 2], ret_got.at[k], ret_sem.at[0, k], ret_sem.at[1, k], owner_of(me, k)
        )

    acc[...] = jnp.zeros_like(acc)

    def forward(i, carry):
        lanes, at = place(i, FORWARD_CHUNK)
        arrived = dot(table[4 * TRIP : 5 * TRIP, :], hot_s[:, lanes])
        weight = basis[:, lanes]
        near_rows = rows[:, lanes].astype(F32)
        found, messages = [], []
        for q in range(FORWARD_CHUNK // 128):
            part = slice(128 * q, 128 * q + 128)
            held = jnp.broadcast_to(shi[at[q], :], (TRIP, 128))
            row = jnp.where(held == 4.0, arrived[:, part], near_rows[:, part])
            found.append(row.astype(BF16))
            messages.append(spread((row * weight[:, part]).astype(BF16), thi[at[q], :], 4))
        all_rows[:, lanes] = jnp.concatenate(found, axis=1)
        acc[...] += dot_cols(jnp.concatenate(messages, axis=1), hot_t[:, lanes])
        return carry

    lax.fori_loop(0, TRIPS // FORWARD_CHUNK, forward, 0)
    agg_t = unstack_groups(acc[...], 4)

    agg = (0.5 * agg_t.astype(BF16).astype(F32)).T.astype(BF16)
    agg_t = agg_t.astype(BF16)
    loads["up"].wait()
    loads["cot"].wait()
    up_w = up[...]
    for b in range(4):
        at = slice(256 * b, 256 * b + 256)
        half = dot(agg[at, :], up_w)
        bent = jnp.tanh(half)
        slope = (1.0 + bent) * (1.0 + half * (1.0 - bent))
        ugrad[at, :] = (cot[at, :].astype(F32) * (0.5 * residual_scale) * slope).astype(BF16)
    target_table[...] = stack_groups(dot_cols(up_w, ugrad[...]).astype(BF16), 4)
    grad_up = dot(agg_t, ugrad[...]).astype(BF16)
    for at in range(NEAR):
        u_sent[at, :, 0:256] = grad_up[chunk_place(at)]

    loads["bv"].wait()
    acc2[...] = jnp.zeros_like(acc2)
    accb[...] = jnp.zeros_like(accb)

    def backward(i, carry):
        lanes, at = place(i, BACKWARD_CHUNK)
        grouped = dot(target_table[...], hot_t[:, lanes])
        weight = basis[:, lanes]
        row = all_rows[:, lanes].astype(F32)
        zero = jnp.zeros((TRIP, 128), F32)
        sources, weights = [], []
        for q in range(BACKWARD_CHUNK // 128):
            part = slice(128 * q, 128 * q + 128)
            gate = pick(grouped[:, part], thi[at[q], :], 4, zero)
            weights.append((gate * row[:, part]).astype(BF16))
            sources.append(spread((gate * weight[:, part]).astype(BF16), shi[at[q], :], 5))
        acc2[...] += dot_cols(jnp.concatenate(sources, axis=1), hot_s[:, lanes])
        accb[0:NB, 0:TRIP] += dot_cols(bv[:, lanes], jnp.concatenate(weights, axis=1))
        return carry

    lax.fori_loop(0, TRIPS // BACKWARD_CHUNK, backward, 0)

    far_grad = acc2[4 * TRIP : 5 * TRIP, :]
    ret_sent[0] = far_grad[:, 0:128].astype(BF16)
    ret_sent[1] = far_grad[:, 128:256].astype(BF16)
    pl.semaphore_wait(pltpu.get_barrier_semaphore(), PEERS + NEAR - 1 + FAR - 1)
    for k in (0, 3, 1, 2):
        ret_copy(k).start()
    state = jnp.concatenate([state_got[k] for k in range(PEERS)], axis=0)
    far_gate = (far_grad * far_slope[...]).astype(BF16)
    own_grad = unstack_groups(acc2[0 : 4 * TRIP, :], 4)
    own_gate = (own_grad * local_slope[...]).astype(BF16)
    loads["edge"].wait()
    grad_down = (dot(own_gate, edge[...]) + dot(far_gate, state)).astype(BF16)
    for at in range(NEAR):
        d_sent[at] = grad_down[chunk_place(at)]
    down_sums.start()
    for at in range(NEAR):
        rest = accb[16 * at : 16 * at + 16, :] if at < 3 else jnp.zeros((16, 128), F32)
        u_sent[at, :, 256:384] = rest.astype(BF16)
    up_sums.start()
    down_sums.second()
    up_sums.second()

    for k in range(PEERS):
        ret_copy(k).wait_recv()
    slot_lane, offset = slot_offsets()
    read = (me - offset >= 0) & (me - offset < N)
    even = jnp.concatenate([ret_got[0].astype(F32), ret_got[2].astype(F32)], axis=1)
    odd = jnp.concatenate([ret_got[1].astype(F32), ret_got[3].astype(F32)], axis=1)
    back = jnp.where((slot_lane & SLOT) == 0, even, odd)
    back = jnp.where(read, back, 0.0).astype(BF16)
    hidden_grad = own_grad + dot(back, hot_list[...])
    gate = (hidden_grad * local_slope[...]).T.astype(BF16)
    loads["down"].wait()
    for b in range(4):
        at = slice(256 * b, 256 * b + 256)
        through = dot(gate[at, :], down[...])
        edge_grad_ref[at, :] = (cot[at, :].astype(F32) * residual_scale + through).astype(BF16)
    for k in range(PEERS):
        ret_copy(k).wait_send()
    down_sums.third()
    up_sums.third()
    down_sums.drain_early()
    up_sums.drain_early()
    down_sums.finish()
    for at in range(NEAR):
        grad_down_ref[chunk_place(at)] = d_done[at].astype(F32)
    up_sums.finish()
    for at in range(NEAR):
        grad_up_ref[chunk_place(at)] = u_done[at, :, 0:256].astype(F32)
    for at in range(3):
        count_rows = min(16, NB - 16 * at)
        grad_basis_ref[16 * at : 16 * at + count_rows, :] = u_done[
            at, 0:count_rows, 256 : 256 + TRIP
        ].astype(F32)
    down_sums.drain()
    up_sums.drain()


def store_kernel(a, b, c, d, a_hbm, b_hbm, c_hbm, d_hbm, sem):
    pairs = [(a.at[256 * i : 256 * i + 256], a_hbm.at[256 * i : 256 * i + 256]) for i in range(4)]
    pairs += [(b, b_hbm), (c, c_hbm), (d, d_hbm)]
    copies = [pltpu.make_async_copy(src, dst, sem.at[at]) for at, (src, dst) in enumerate(pairs)]
    for copy in copies:
        copy.start()
    for copy in copies:
        copy.wait()


def per_device(
    edge_state,
    cotangent,
    basis_values,
    down_weight,
    basis_weight,
    up_weight,
    triplet_source,
    triplet_target,
    block_valid,
    send_lists,
):
    hbm = pl.BlockSpec(memory_space=pltpu.HBM)
    vmem = pl.BlockSpec(memory_space=pltpu.VMEM)
    dma = pltpu.SemaphoreType.DMA
    out_shape = (
        jax.ShapeDtypeStruct((E, D), BF16),
        jax.ShapeDtypeStruct((TRIP, D), F32),
        jax.ShapeDtypeStruct((NB, TRIP), F32),
        jax.ShapeDtypeStruct((TRIP, D), F32),
    )
    args = (
        edge_state,
        cotangent,
        basis_values,
        down_weight.T,
        basis_weight,
        up_weight,
        triplet_source.reshape(64, 128),
        triplet_target.reshape(64, 128),
        block_valid.reshape(1, 128),
        send_lists,
    )
    args = [pltpu.with_memory_space_constraint(arg, pltpu.HBM) for arg in args]
    edges, cots, values, downs, bws, ups, sources, targets, counts, lists = args
    passed = (
        ((PEERS * SLOT, E), BF16),
        ((LO, TRIPS), BF16),
        ((LO, TRIPS), BF16),
        ((TRIP, TRIPS), F32),
        ((TRIP, TRIPS), BF16),
        ((5 * TRIP, LO), BF16),
        ((64, 128), F32),
        ((64, 128), F32),
        ((TRIP, E), F32),
        ((TRIP, LO), F32),
        ((PEERS, SLOT, D), BF16),
    )
    held = pl.pallas_call(
        gather_kernel,
        out_shape=[jax.ShapeDtypeStruct(*one) for one in passed],
        in_specs=[hbm] * 8,
        out_specs=[vmem] * len(passed),
        scratch_shapes=[
            pltpu.VMEM((E, D), BF16),
            pltpu.VMEM((NB, TRIPS), BF16),
            pltpu.VMEM((TRIP, D), BF16),
            pltpu.VMEM((NB, TRIP), BF16),
            pltpu.VMEM((64, 128), I32),
            pltpu.VMEM((64, 128), I32),
            pltpu.VMEM((1, 128), I32),
            pltpu.VMEM((PEERS, SLOT), I32),
            pltpu.VMEM((LO, 128), BF16),
            pltpu.VMEM((64, 128), F32),
            pltpu.VMEM((64, 128), F32),
            pltpu.VMEM((PEERS, SLOT, D), BF16),
            dma((8,)),
            dma((2, PEERS)),
        ],
        compiler_params=pltpu.CompilerParams(
            collective_id=0, has_side_effects=True, vmem_limit_bytes=40 * 1024 * 1024
        ),
    )(edges, values, downs, bws, sources, targets, counts, lists)
    results = pl.pallas_call(
        triplet_kernel,
        out_shape=out_shape,
        in_specs=[hbm] * 5 + [vmem] * len(passed),
        out_specs=(vmem,) * 4,
        scratch_shapes=[
            pltpu.VMEM((E, D), BF16),
            pltpu.VMEM((E, D), BF16),
            pltpu.VMEM((NB, TRIPS), BF16),
            pltpu.VMEM((TRIP, D), BF16),
            pltpu.VMEM((TRIP, D), BF16),
            pltpu.VMEM((TRIP, TRIPS), BF16),
            pltpu.VMEM((4 * TRIP, LO), BF16),
            pltpu.VMEM((4 * TRIP, LO), F32),
            pltpu.VMEM((5 * TRIP, LO), F32),
            pltpu.VMEM((48, 128), F32),
            pltpu.VMEM((E, D), BF16),
            pltpu.VMEM((2, TRIP, 128), BF16),
            pltpu.VMEM((PEERS, TRIP, 128), BF16),
            pltpu.VMEM((NEAR, 16, 384), BF16),
            pltpu.VMEM((NEAR - 1, 16, 384), BF16),
            pltpu.VMEM((FAR, 16, 384), BF16),
            pltpu.VMEM((NEAR, 16, 384), BF16),
            pltpu.VMEM((NEAR, 16, 256), BF16),
            pltpu.VMEM((NEAR - 1, 16, 256), BF16),
            pltpu.VMEM((FAR, 16, 256), BF16),
            pltpu.VMEM((NEAR, 16, 256), BF16),
            dma((5,)),
            dma((2, PEERS)),
            dma((6, NEAR - 1)),
            dma((6, NEAR - 1)),
        ],
        compiler_params=pltpu.CompilerParams(
            collective_id=1, has_side_effects=True, vmem_limit_bytes=40 * 1024 * 1024
        ),
    )(edges, cots, values, downs, ups, *held)
    edge_grad, grad_down, grad_basis, grad_up = pl.pallas_call(
        store_kernel,
        out_shape=out_shape,
        in_specs=[vmem] * 4,
        out_specs=(hbm,) * 4,
        scratch_shapes=[dma((7,))],
        compiler_params=pltpu.CompilerParams(vmem_limit_bytes=1024 * 1024),
    )(*results)
    return edge_grad, grad_down.T, grad_basis, grad_up


def solution(mesh):
    return jax.shard_map(
        per_device,
        mesh=mesh,
        in_specs=(
            P(("dp", "graph"), None),
            P(("dp", "graph"), None),
            P(None, ("dp", "graph")),
            P(),
            P(),
            P(),
            P(("dp", "graph")),
            P(("dp", "graph")),
            P(("dp", "graph")),
            P(("dp", "graph"), None),
        ),
        out_specs=(P(("dp", "graph"), None), P("dp", None), P("dp", None), P("dp", None)),
        check_vma=False,
    )
```

time: 49.5 us -> 48.5 us (0.980)
  Pallas kernels: 48.7 us -> 47.7 us
    pallas_call x1 -> x2, Pallas kernels: 47.6 us -> 46.6 us  [the longest x1 28.2 us: per_device(): pl.pallas_call(triplet_kernel, out_shape=out_shape, in_specs=[hbm] * 5 +...]
where the time goes in v3:
time: 48.5 us; the launch traced here: 48.4 us
  Pallas kernels  47.7 us (98%)
  between operations  0.65 us (1%)
    pallas_call x1, Pallas kernels, per_device(): pl.pallas_call(triplet_kernel, out_shape=out_shape, in_specs=[hbm] * 5 +...  28.2 us
    pallas_call x1, Pallas kernels, per_device(): pl.pallas_call(gather_kernel, out_shape=[jax.ShapeDtypeStruct(*one) for o...  18.4 us
    pallas_call x1, Pallas kernels, per_device(): pl.pallas_call(store_kernel, out_shape=out_shape, in_specs=[vmem] * 4, ou...  1.11 us

profile of v3, /device:TPU:6, one launch (start us, length us, event | category | flops | bytes accessed | tf_op | source)
XLA Modules:
  0.0 48.4 jit_solution(9764332732517553443)
XLA Ops:
  0.6 18.4 %shard_map.129 = (bf16[256,1024]{1,0:T(8,128)(2,1)S(1)}, bf16[256,8192]{1,0:T(8,128)(2,1)S(1)}, bf16[256,8192]{1,0:T(8,128)(2,1)S(1)}, f32[64,8192]{1,0:T(8,128)...) custom-call(bf16[1024,512]{1,0:T(8,128)(2,1)} %edge_hbm.3, ...), custom_call_target="tpu_custom_call" | custom-call | tf_op jit(solution)/shard_map/pallas_call | solution.py:611
  19.1 28.2 %shard_map.130 = (bf16[1024,512]{1,0:T(8,128)(2,1)S(1)}, f32[64,512]{1,0:T(8,128)S(1)}, f32[42,64]{1,0:T(8,128)S(1)}, f32[64,512]{1,0:T(8,128)S(1)}) custom-call(bf16[1024,512]{1,0:T(8,128)(2,1)} %edge_hbm.3, bf16[1024,512]{1,0:T(8,128)(2,1)} %cot_hbm.1, bf16[42,8192]{1,0:T(8,128)(2,1)} %bv_hbm.3, bf16[64,512]{1,0:T(8,128)(2,1)} %bitcast.6, ...), custom_call_target="tpu_custom_call" | custom-call | tf_op jit(solution)/shard_map/pallas_call | solution.py:636
  47.3 1.1 %shard_map.131 = (bf16[1024,512]{1,0:T(8,128)(2,1)}, f32[64,512]{1,0:T(8,128)}, f32[42,64]{1,0:T(8,128)}, f32[64,512]{1,0:T(8,128)}) custom-call(bf16[1024,512]{1,0:T(8,128)(2,1)S(1)} %get-tuple-element.34.a, f32[64,512]{1,0:T(8,128)S(1)} %get-tuple-element.35.b, f32[42,64]{1,0:T(8,128)S(1)} %get-tuple-element.36.c, f32[64,512]{1,0:T(8,128)S(1)} %get-tuple-element.37.d), custom_call_target="tpu_custom_call" | custom-call | tf_op jit(solution)/shard_map/pallas_call | solution.py:672

commit v4 on v3

--- a/solution.py
+++ b/solution.py
@@ -221,29 +221,39 @@
     return slot_lane, offset
 
 
-def gather_kernel(
+def joined(got, slot_lane):
+    even = jnp.concatenate([got[0].astype(F32), got[2].astype(F32)], axis=1)
+    odd = jnp.concatenate([got[1].astype(F32), got[3].astype(F32)], axis=1)
+    return jnp.where((slot_lane & SLOT) == 0, even, odd)
+
+
+def forward_kernel(
     edge_hbm,
+    cot_hbm,
     bv_hbm,
     down_hbm,
     bw_hbm,
+    up_hbm,
     source_hbm,
     target_hbm,
     count_hbm,
     lists_hbm,
+    edge,
+    cot,
+    bv,
+    down,
+    up,
     hot_list,
     hot_s,
     hot_t,
     basis,
     rows,
-    table,
+    acc,
     shi,
     thi,
     local_slope,
     far_slope,
     state_got,
-    edge,
-    bv,
-    down,
     bw,
     source,
     target,
@@ -252,8 +262,12 @@
     iota,
     slo,
     tlo,
+    table,
+    fwd_sent,
+    fwd_got,
     state_sent,
     load_sem,
+    fwd_sem,
     state_sem,
 ):
     me = lax.axis_index("graph")
@@ -270,8 +284,15 @@
             ("target", target_hbm, target),
             ("bw", bw_hbm, bw),
             ("bv", bv_hbm, bv),
+            ("up", up_hbm, up),
+            ("cot", cot_hbm, cot),
         ),
     )
+
+    def fwd_copy(k):
+        return remote(
+            fwd_sent.at[k // 2], fwd_got.at[k], fwd_sem.at[0, k], fwd_sem.at[1, k], reader_of(me, k)
+        )
 
     def state_copy(k):
         return remote(
@@ -296,20 +317,24 @@
             lanes + float(128 * b) == number, 1.0, 0.0
         ).astype(BF16)
 
+    loads["down"].wait()
     loads["edge"].wait()
+    projected = dot_cols(down[...], edge[...])
+    sigma = sigmoid(projected)
+    hidden = (projected * sigma).astype(BF16)
+    chosen = dot_cols(hidden, hot_list[...]).astype(BF16)
+    fwd_sent[0] = chosen[:, 0:128]
+    fwd_sent[1] = chosen[:, 128:256]
+    pl.semaphore_wait(pltpu.get_barrier_semaphore(), PEERS)
+    for k in (0, 3, 1, 2):
+        fwd_copy(k).start()
+    local_slope[...] = sigma * (1.0 + projected * (1.0 - sigma))
+    table[0 : 4 * TRIP, :] = stack_groups(hidden, 4)
     listed_rows = dot(hot_list[...], edge[...]).astype(BF16)
     for k in range(PEERS):
         state_sent[k] = listed_rows[SLOT * k : SLOT * (k + 1), :]
-    pl.semaphore_wait(pltpu.get_barrier_semaphore(), PEERS)
     for k in (0, 3, 1, 2):
         state_copy(k).start()
-
-    loads["down"].wait()
-    projected = dot_cols(down[...], edge[...])
-    sigma = sigmoid(projected)
-    local_slope[...] = sigma * (1.0 + projected * (1.0 - sigma))
-    hidden = (projected * sigma).astype(BF16)
-    table[0 : 4 * TRIP, :] = stack_groups(hidden, 4)
 
     loads["count"].wait()
     shape = (64, 128)
@@ -347,32 +372,55 @@
 
     lax.fori_loop(0, TRIPS // PREPARE_CHUNK, prepare, 0)
 
+    slot_lane, offset = slot_offsets()
+    named = (me + offset >= 0) & (me + offset < N)
+    for k in range(PEERS):
+        fwd_copy(k).wait_recv()
+    table[4 * TRIP : 5 * TRIP, :] = jnp.where(named, joined(fwd_got, slot_lane), 0.0).astype(BF16)
+
+    acc[...] = jnp.zeros_like(acc)
+
+    def forward(i, carry):
+        lanes, at = place(i, FORWARD_CHUNK)
+        arrived = dot(table[4 * TRIP : 5 * TRIP, :], hot_s[:, lanes])
+        weight = basis[:, lanes]
+        near_rows = rows[:, lanes].astype(F32)
+        found, messages = [], []
+        for q in range(FORWARD_CHUNK // 128):
+            part = slice(128 * q, 128 * q + 128)
+            held = jnp.broadcast_to(shi[at[q], :], (TRIP, 128))
+            row = jnp.where(held == 4.0, arrived[:, part], near_rows[:, part])
+            found.append(row.astype(BF16))
+            messages.append(spread((row * weight[:, part]).astype(BF16), thi[at[q], :], 4))
+        rows[:, lanes] = jnp.concatenate(found, axis=1)
+        acc[...] += dot_cols(jnp.concatenate(messages, axis=1), hot_t[:, lanes])
+        return carry
+
+    lax.fori_loop(0, TRIPS // FORWARD_CHUNK, forward, 0)
+
     for k in range(PEERS):
         state_copy(k).wait_recv()
-    offset = slot_offsets()[1]
-    named = (me + offset >= 0) & (me + offset < N)
     state = jnp.concatenate([state_got[k] for k in range(PEERS)], axis=0)
-    far_projected = dot_cols(down[...], state)
-    sigma = sigmoid(far_projected)
-    slope = sigma * (1.0 + far_projected * (1.0 - sigma))
-    far_slope[...] = jnp.where(named, slope, 0.0)
-    table[4 * TRIP : 5 * TRIP, :] = jnp.where(named, far_projected * sigma, 0.0).astype(BF16)
+    far_slope[...] = jnp.where(named, slope_of(dot_cols(down[...], state)), 0.0)
+    for name in ("up", "cot"):
+        loads[name].wait()
     for k in range(PEERS):
+        fwd_copy(k).wait_send()
         state_copy(k).wait_send()
 
 
-def triplet_kernel(
-    edge_hbm,
-    cot_hbm,
-    bv_hbm,
-    down_hbm,
-    up_hbm,
+def backward_kernel(
+    edge,
+    cot,
+    bv,
+    down,
+    up,
     hot_list,
     hot_s,
     hot_t,
     basis,
     rows,
-    table,
+    acc,
     shi,
     thi,
     local_slope,
@@ -382,14 +430,7 @@
     grad_down_ref,
     grad_basis_ref,
     grad_up_ref,
-    edge,
-    cot,
-    bv,
-    down,
-    up,
-    all_rows,
     target_table,
-    acc,
     acc2,
     accb,
     ugrad,
@@ -403,7 +444,6 @@
     d_got,
     d_far,
     d_done,
-    load_sem,
     ret_sem,
     u_sem,
     d_sem,
@@ -415,16 +455,6 @@
         greet(near_peer(me, step)[1])
     for k in range(PEERS):
         greet(owner_of(me, k))
-    loads = start_loads(
-        load_sem,
-        (
-            ("up", up_hbm, up),
-            ("cot", cot_hbm, cot),
-            ("bv", bv_hbm, bv),
-            ("down", down_hbm, down),
-            ("edge", edge_hbm, edge),
-        ),
-    )
     up_sums = Reduction(me, u_sent, u_got, u_far, u_done, u_sem)
     down_sums = Reduction(me, d_sent, d_got, d_far, d_done, d_sem)
 
@@ -433,31 +463,10 @@
             ret_sent.at[k // 2], ret_got.at[k], ret_sem.at[0, k], ret_sem.at[1, k], owner_of(me, k)
         )
 
-    acc[...] = jnp.zeros_like(acc)
-
-    def forward(i, carry):
-        lanes, at = place(i, FORWARD_CHUNK)
-        arrived = dot(table[4 * TRIP : 5 * TRIP, :], hot_s[:, lanes])
-        weight = basis[:, lanes]
-        near_rows = rows[:, lanes].astype(F32)
-        found, messages = [], []
-        for q in range(FORWARD_CHUNK // 128):
-            part = slice(128 * q, 128 * q + 128)
-            held = jnp.broadcast_to(shi[at[q], :], (TRIP, 128))
-            row = jnp.where(held == 4.0, arrived[:, part], near_rows[:, part])
-            found.append(row.astype(BF16))
-            messages.append(spread((row * weight[:, part]).astype(BF16), thi[at[q], :], 4))
-        all_rows[:, lanes] = jnp.concatenate(found, axis=1)
-        acc[...] += dot_cols(jnp.concatenate(messages, axis=1), hot_t[:, lanes])
-        return carry
-
-    lax.fori_loop(0, TRIPS // FORWARD_CHUNK, forward, 0)
     agg_t = unstack_groups(acc[...], 4)
 
     agg = (0.5 * agg_t.astype(BF16).astype(F32)).T.astype(BF16)
     agg_t = agg_t.astype(BF16)
-    loads["up"].wait()
-    loads["cot"].wait()
     up_w = up[...]
     for b in range(4):
         at = slice(256 * b, 256 * b + 256)
@@ -470,7 +479,6 @@
     for at in range(NEAR):
         u_sent[at, :, 0:256] = grad_up[chunk_place(at)]
 
-    loads["bv"].wait()
     acc2[...] = jnp.zeros_like(acc2)
     accb[...] = jnp.zeros_like(accb)
 
@@ -478,7 +486,7 @@
         lanes, at = place(i, BACKWARD_CHUNK)
         grouped = dot(target_table[...], hot_t[:, lanes])
         weight = basis[:, lanes]
-        row = all_rows[:, lanes].astype(F32)
+        row = rows[:, lanes].astype(F32)
         zero = jnp.zeros((TRIP, 128), F32)
         sources, weights = [], []
         for q in range(BACKWARD_CHUNK // 128):
@@ -493,24 +501,23 @@
     lax.fori_loop(0, TRIPS // BACKWARD_CHUNK, backward, 0)
 
     far_grad = acc2[4 * TRIP : 5 * TRIP, :]
-    ret_sent[0] = far_grad[:, 0:128].astype(BF16)
-    ret_sent[1] = far_grad[:, 128:256].astype(BF16)
-    pl.semaphore_wait(pltpu.get_barrier_semaphore(), PEERS + NEAR - 1 + FAR - 1)
-    for k in (0, 3, 1, 2):
-        ret_copy(k).start()
     state = jnp.concatenate([state_got[k] for k in range(PEERS)], axis=0)
     far_gate = (far_grad * far_slope[...]).astype(BF16)
     own_grad = unstack_groups(acc2[0 : 4 * TRIP, :], 4)
     own_gate = (own_grad * local_slope[...]).astype(BF16)
-    loads["edge"].wait()
     grad_down = (dot(own_gate, edge[...]) + dot(far_gate, state)).astype(BF16)
     for at in range(NEAR):
         d_sent[at] = grad_down[chunk_place(at)]
+    pl.semaphore_wait(pltpu.get_barrier_semaphore(), PEERS + NEAR - 1 + FAR - 1)
     down_sums.start()
     for at in range(NEAR):
         rest = accb[16 * at : 16 * at + 16, :] if at < 3 else jnp.zeros((16, 128), F32)
         u_sent[at, :, 256:384] = rest.astype(BF16)
+    ret_sent[0] = far_grad[:, 0:128].astype(BF16)
+    ret_sent[1] = far_grad[:, 128:256].astype(BF16)
     up_sums.start()
+    for k in (0, 3, 1, 2):
+        ret_copy(k).start()
     down_sums.second()
     up_sums.second()
 
@@ -518,13 +525,10 @@
         ret_copy(k).wait_recv()
     slot_lane, offset = slot_offsets()
     read = (me - offset >= 0) & (me - offset < N)
-    even = jnp.concatenate([ret_got[0].astype(F32), ret_got[2].astype(F32)], axis=1)
-    odd = jnp.concatenate([ret_got[1].astype(F32), ret_got[3].astype(F32)], axis=1)
-    back = jnp.where((slot_lane & SLOT) == 0, even, odd)
+    back = joined(ret_got, slot_lane)
     back = jnp.where(read, back, 0.0).astype(BF16)
     hidden_grad = own_grad + dot(back, hot_list[...])
     gate = (hidden_grad * local_slope[...]).T.astype(BF16)
-    loads["down"].wait()
     for b in range(4):
         at = slice(256 * b, 256 * b + 256)
         through = dot(gate[at, :], down[...])
@@ -594,14 +598,18 @@
         send_lists,
     )
     args = [pltpu.with_memory_space_constraint(arg, pltpu.HBM) for arg in args]
-    edges, cots, values, downs, bws, ups, sources, targets, counts, lists = args
     passed = (
+        ((E, D), BF16),
+        ((E, D), BF16),
+        ((NB, TRIPS), BF16),
+        ((TRIP, D), BF16),
+        ((TRIP, D), BF16),
         ((PEERS * SLOT, E), BF16),
         ((LO, TRIPS), BF16),
         ((LO, TRIPS), BF16),
         ((TRIP, TRIPS), F32),
         ((TRIP, TRIPS), BF16),
-        ((5 * TRIP, LO), BF16),
+        ((4 * TRIP, LO), F32),
         ((64, 128), F32),
         ((64, 128), F32),
         ((TRIP, E), F32),
@@ -609,14 +617,11 @@
         ((PEERS, SLOT, D), BF16),
     )
     held = pl.pallas_call(
-        gather_kernel,
+        forward_kernel,
         out_shape=[jax.ShapeDtypeStruct(*one) for one in passed],
-        in_specs=[hbm] * 8,
+        in_specs=[hbm] * 10,
         out_specs=[vmem] * len(passed),
         scratch_shapes=[
-            pltpu.VMEM((E, D), BF16),
-            pltpu.VMEM((NB, TRIPS), BF16),
-            pltpu.VMEM((TRIP, D), BF16),
             pltpu.VMEM((NB, TRIP), BF16),
             pltpu.VMEM((64, 128), I32),
             pltpu.VMEM((64, 128), I32),
@@ -625,28 +630,25 @@
             pltpu.VMEM((LO, 128), BF16),
             pltpu.VMEM((64, 128), F32),
             pltpu.VMEM((64, 128), F32),
+            pltpu.VMEM((5 * TRIP, LO), BF16),
+            pltpu.VMEM((2, TRIP, 128), BF16),
+            pltpu.VMEM((PEERS, TRIP, 128), BF16),
             pltpu.VMEM((PEERS, SLOT, D), BF16),
-            dma((8,)),
+            dma((10,)),
+            dma((2, PEERS)),
             dma((2, PEERS)),
         ],
         compiler_params=pltpu.CompilerParams(
-            collective_id=0, has_side_effects=True, vmem_limit_bytes=40 * 1024 * 1024
+            collective_id=0, has_side_effects=True, vmem_limit_bytes=36 * 1024 * 1024
         ),
-    )(edges, values, downs, bws, sources, targets, counts, lists)
+    )(*args)
     results = pl.pallas_call(
-        triplet_kernel,
+        backward_kernel,
         out_shape=out_shape,
-        in_specs=[hbm] * 5 + [vmem] * len(passed),
+        in_specs=[vmem] * len(passed),
         out_specs=(vmem,) * 4,
         scratch_shapes=[
-            pltpu.VMEM((E, D), BF16),
-            pltpu.VMEM((E, D), BF16),
-            pltpu.VMEM((NB, TRIPS), BF16),
-            pltpu.VMEM((TRIP, D), BF16),
-            pltpu.VMEM((TRIP, D), BF16),
-            pltpu.VMEM((TRIP, TRIPS), BF16),
             pltpu.VMEM((4 * TRIP, LO), BF16),
-            pltpu.VMEM((4 * TRIP, LO), F32),
             pltpu.VMEM((5 * TRIP, LO), F32),
             pltpu.VMEM((48, 128), F32),
             pltpu.VMEM((E, D), BF16),
@@ -660,15 +662,14 @@
             pltpu.VMEM((NEAR - 1, 16, 256), BF16),
             pltpu.VMEM((FAR, 16, 256), BF16),
             pltpu.VMEM((NEAR, 16, 256), BF16),
-            dma((5,)),
             dma((2, PEERS)),
             dma((6, NEAR - 1)),
             dma((6, NEAR - 1)),
         ],
         compiler_params=pltpu.CompilerParams(
-            collective_id=1, has_side_effects=True, vmem_limit_bytes=40 * 1024 * 1024
+            collective_id=1, has_side_effects=True, vmem_limit_bytes=36 * 1024 * 1024
         ),
-    )(edges, cots, values, downs, ups, *held)
+    )(*held)
     edge_grad, grad_down, grad_basis, grad_up = pl.pallas_call(
         store_kernel,
         out_shape=out_shape,

time: 48.5 us -> 47.6 us (0.981)
  Pallas kernels: 47.7 us -> 46.5 us
    pallas_call x2, Pallas kernels: 46.6 us -> 45.3 us  [the longest x1 25.6 us: per_device(): pl.pallas_call(backward_kernel, out_shape=out_shape, in_specs=[vmem] * le...]
where the time goes in v4:
time: 47.6 us; the launch traced here: 47.1 us
  Pallas kernels  46.5 us (98%)
  between operations  0.65 us (1%)
    pallas_call x1, Pallas kernels, per_device(): pl.pallas_call(backward_kernel, out_shape=out_shape, in_specs=[vmem] * le...  25.6 us
    pallas_call x1, Pallas kernels, per_device(): pl.pallas_call(forward_kernel, out_shape=[jax.ShapeDtypeStruct(*one) for...  19.8 us
    pallas_call x1, Pallas kernels, per_device(): pl.pallas_call(store_kernel, out_shape=out_shape, in_specs=[vmem] * 4, ou...  1.11 us

profile of v4, /device:TPU:6, one launch (start us, length us, event | category | flops | bytes accessed | tf_op | source)
XLA Modules:
  0.0 47.1 jit_solution(1230539286779243751)
XLA Ops:
  0.6 19.8 %shard_map.129 = (bf16[1024,512]{1,0:T(8,128)(2,1)S(1)}, bf16[1024,512]{1,0:T(8,128)(2,1)S(1)}, bf16[42,8192]{1,0:T(8,128)(2,1)S(1)}, bf16[64,512]{1,0:T(8,128)(...) custom-call(bf16[1024,512]{1,0:T(8,128)(2,1)} %edge_hbm.1, ...), custom_call_target="tpu_custom_call" | custom-call | tf_op jit(solution)/shard_map/pallas_call | solution.py:619
  20.4 25.6 %shard_map.130 = (bf16[1024,512]{1,0:T(8,128)(2,1)S(1)}, f32[64,512]{1,0:T(8,128)S(1)}, f32[42,64]{1,0:T(8,128)S(1)}, f32[64,512]{1,0:T(8,128)S(1)}) custom-call(bf16[1024,512]{1,0:T(8,128)(2,1)S(1)} %get-tuple-element.28.edge, bf16[1024,512]{1,0:T(8,128)(2,1)S(1)} %get-tuple-element.29.cot, bf16[42,8192]{1,0:T(8,128)(2,1)S(1)} %get-tuple-element.30.bv, ...), custom_call_target="tpu_custom_call" | custom-call | tf_op jit(solution)/shard_map/pallas_call | solution.py:645
  46.0 1.1 %shard_map.131 = (bf16[1024,512]{1,0:T(8,128)(2,1)}, f32[64,512]{1,0:T(8,128)}, f32[42,64]{1,0:T(8,128)}, f32[64,512]{1,0:T(8,128)}) custom-call(bf16[1024,512]{1,0:T(8,128)(2,1)S(1)} %get-tuple-element.44.a, f32[64,512]{1,0:T(8,128)S(1)} %get-tuple-element.45.b, f32[42,64]{1,0:T(8,128)S(1)} %get-tuple-element.46.c, f32[64,512]{1,0:T(8,128)S(1)} %get-tuple-element.47.d), custom_call_target="tpu_custom_call" | custom-call | tf_op jit(solution)/shard_map/pallas_call | solution.py:673

commit v5 on v4

--- a/solution.py
+++ b/solution.py
@@ -436,17 +436,12 @@
     ugrad,
     ret_sent,
     ret_got,
-    u_sent,
-    u_got,
-    u_far,
-    u_done,
-    d_sent,
-    d_got,
-    d_far,
-    d_done,
+    sent,
+    got,
+    far,
+    done,
     ret_sem,
-    u_sem,
-    d_sem,
+    sum_sem,
 ):
     me = lax.axis_index("graph")
     for step in FAR_ORDER:
@@ -455,8 +450,7 @@
         greet(near_peer(me, step)[1])
     for k in range(PEERS):
         greet(owner_of(me, k))
-    up_sums = Reduction(me, u_sent, u_got, u_far, u_done, u_sem)
-    down_sums = Reduction(me, d_sent, d_got, d_far, d_done, d_sem)
+    sums = Reduction(me, sent, got, far, done, sum_sem)
 
     def ret_copy(k):
         return remote(
@@ -477,7 +471,7 @@
     target_table[...] = stack_groups(dot_cols(up_w, ugrad[...]).astype(BF16), 4)
     grad_up = dot(agg_t, ugrad[...]).astype(BF16)
     for at in range(NEAR):
-        u_sent[at, :, 0:256] = grad_up[chunk_place(at)]
+        sent[at, :, 256:512] = grad_up[chunk_place(at)]
 
     acc2[...] = jnp.zeros_like(acc2)
     accb[...] = jnp.zeros_like(accb)
@@ -507,19 +501,16 @@
     own_gate = (own_grad * local_slope[...]).astype(BF16)
     grad_down = (dot(own_gate, edge[...]) + dot(far_gate, state)).astype(BF16)
     for at in range(NEAR):
-        d_sent[at] = grad_down[chunk_place(at)]
+        sent[at, :, 0:256] = grad_down[chunk_place(at)]
+        rest = accb[16 * at : 16 * at + 16, :] if at < 3 else jnp.zeros((16, 128), F32)
+        sent[at, :, 512:640] = rest.astype(BF16)
     pl.semaphore_wait(pltpu.get_barrier_semaphore(), PEERS + NEAR - 1 + FAR - 1)
-    down_sums.start()
-    for at in range(NEAR):
-        rest = accb[16 * at : 16 * at + 16, :] if at < 3 else jnp.zeros((16, 128), F32)
-        u_sent[at, :, 256:384] = rest.astype(BF16)
+    sums.start()
     ret_sent[0] = far_grad[:, 0:128].astype(BF16)
     ret_sent[1] = far_grad[:, 128:256].astype(BF16)
-    up_sums.start()
     for k in (0, 3, 1, 2):
         ret_copy(k).start()
-    down_sums.second()
-    up_sums.second()
+    sums.second()
 
     for k in range(PEERS):
         ret_copy(k).wait_recv()
@@ -535,23 +526,18 @@
         edge_grad_ref[at, :] = (cot[at, :].astype(F32) * residual_scale + through).astype(BF16)
     for k in range(PEERS):
         ret_copy(k).wait_send()
-    down_sums.third()
-    up_sums.third()
-    down_sums.drain_early()
-    up_sums.drain_early()
-    down_sums.finish()
+    sums.third()
+    sums.drain_early()
+    sums.finish()
     for at in range(NEAR):
-        grad_down_ref[chunk_place(at)] = d_done[at].astype(F32)
-    up_sums.finish()
-    for at in range(NEAR):
-        grad_up_ref[chunk_place(at)] = u_done[at, :, 0:256].astype(F32)
+        grad_down_ref[chunk_place(at)] = done[at, :, 0:256].astype(F32)
+        grad_up_ref[chunk_place(at)] = done[at, :, 256:512].astype(F32)
     for at in range(3):
         count_rows = min(16, NB - 16 * at)
-        grad_basis_ref[16 * at : 16 * at + count_rows, :] = u_done[
-            at, 0:count_rows, 256 : 256 + TRIP
+        grad_basis_ref[16 * at : 16 * at + count_rows, :] = done[
+            at, 0:count_rows, 512 : 512 + TRIP
         ].astype(F32)
-    down_sums.drain()
-    up_sums.drain()
+    sums.drain()
 
 
 def store_kernel(a, b, c, d, a_hbm, b_hbm, c_hbm, d_hbm, sem):
@@ -654,16 +640,11 @@
             pltpu.VMEM((E, D), BF16),
             pltpu.VMEM((2, TRIP, 128), BF16),
             pltpu.VMEM((PEERS, TRIP, 128), BF16),
-            pltpu.VMEM((NEAR, 16, 384), BF16),
-            pltpu.VMEM((NEAR - 1, 16, 384), BF16),
-            pltpu.VMEM((FAR, 16, 384), BF16),
-            pltpu.VMEM((NEAR, 16, 384), BF16),
-            pltpu.VMEM((NEAR, 16, 256), BF16),
-            pltpu.VMEM((NEAR - 1, 16, 256), BF16),
-            pltpu.VMEM((FAR, 16, 256), BF16),
-            pltpu.VMEM((NEAR, 16, 256), BF16),
+            pltpu.VMEM((NEAR, 16, 640), BF16),
+            pltpu.VMEM((NEAR - 1, 16, 640), BF16),
+            pltpu.VMEM((FAR, 16, 640), BF16),
+            pltpu.VMEM((NEAR, 16, 640), BF16),
             dma((2, PEERS)),
-            dma((6, NEAR - 1)),
             dma((6, NEAR - 1)),
         ],
         compiler_params=pltpu.CompilerParams(

time: 47.6 us -> 46.1 us (0.968)
  Pallas kernels: 46.5 us -> 45.3 us
    pallas_call x1, Pallas kernels: 25.6 us -> 24.3 us  [per_device(): pl.pallas_call(backward_kernel, out_shape=out_shape, in_specs=[vmem] * le...]
where the time goes in v5:
time: 46.1 us; the launch traced here: 45.9 us
  Pallas kernels  45.3 us (98%)
  between operations  0.65 us (1%)
    pallas_call x1, Pallas kernels, per_device(): pl.pallas_call(backward_kernel, out_shape=out_shape, in_specs=[vmem] * le...  24.3 us
    pallas_call x1, Pallas kernels, per_device(): pl.pallas_call(forward_kernel, out_shape=[jax.ShapeDtypeStruct(*one) for...  19.8 us
    pallas_call x1, Pallas kernels, per_device(): pl.pallas_call(store_kernel, out_shape=out_shape, in_specs=[vmem] * 4, ou...  1.11 us

profile of v5, /device:TPU:6, one launch (start us, length us, event | category | flops | bytes accessed | tf_op | source)
XLA Modules:
  0.0 45.9 jit_solution(17826340639626047088)
XLA Ops:
  0.6 19.8 %shard_map.129 = (bf16[1024,512]{1,0:T(8,128)(2,1)S(1)}, bf16[1024,512]{1,0:T(8,128)(2,1)S(1)}, bf16[42,8192]{1,0:T(8,128)(2,1)S(1)}, bf16[64,512]{1,0:T(8,128)(...) custom-call(bf16[1024,512]{1,0:T(8,128)(2,1)} %edge_hbm.1, ...), custom_call_target="tpu_custom_call" | custom-call | tf_op jit(solution)/shard_map/pallas_call | solution.py:605
  20.4 24.3 %shard_map.130 = (bf16[1024,512]{1,0:T(8,128)(2,1)S(1)}, f32[64,512]{1,0:T(8,128)S(1)}, f32[42,64]{1,0:T(8,128)S(1)}, f32[64,512]{1,0:T(8,128)S(1)}) custom-call(bf16[1024,512]{1,0:T(8,128)(2,1)S(1)} %get-tuple-element.28.edge, bf16[1024,512]{1,0:T(8,128)(2,1)S(1)} %get-tuple-element.29.cot, bf16[42,8192]{1,0:T(8,128)(2,1)S(1)} %get-tuple-element.30.bv, ...), custom_call_target="tpu_custom_call" | custom-call | tf_op jit(solution)/shard_map/pallas_call | solution.py:631
  44.8 1.1 %shard_map.131 = (bf16[1024,512]{1,0:T(8,128)(2,1)}, f32[64,512]{1,0:T(8,128)}, f32[42,64]{1,0:T(8,128)}, f32[64,512]{1,0:T(8,128)}) custom-call(bf16[1024,512]{1,0:T(8,128)(2,1)S(1)} %get-tuple-element.44.a, f32[64,512]{1,0:T(8,128)S(1)} %get-tuple-element.45.b, f32[42,64]{1,0:T(8,128)S(1)} %get-tuple-element.46.c, f32[64,512]{1,0:T(8,128)S(1)} %get-tuple-element.47.d), custom_call_target="tpu_custom_call" | custom-call | tf_op jit(solution)/shard_map/pallas_call | solution.py:654

commit v6 on v5

--- a/solution.py
+++ b/solution.py
@@ -508,9 +508,9 @@
     sums.start()
     ret_sent[0] = far_grad[:, 0:128].astype(BF16)
     ret_sent[1] = far_grad[:, 128:256].astype(BF16)
+    sums.second()
     for k in (0, 3, 1, 2):
         ret_copy(k).start()
-    sums.second()
 
     for k in range(PEERS):
         ret_copy(k).wait_recv()

time: 46.1 us -> 47.5 us (1.030)
  Pallas kernels: 45.3 us -> 46.7 us
    pallas_call x1, Pallas kernels: 24.3 us -> 25.8 us  [per_device(): pl.pallas_call(backward_kernel, out_shape=out_shape, in_specs=[vmem] * le...]
where the time goes in v6:
time: 47.5 us; the launch traced here: 47.3 us
  Pallas kernels  46.7 us (98%)
  between operations  0.65 us (1%)
    pallas_call x1, Pallas kernels, per_device(): pl.pallas_call(backward_kernel, out_shape=out_shape, in_specs=[vmem] * le...  25.8 us
    pallas_call x1, Pallas kernels, per_device(): pl.pallas_call(forward_kernel, out_shape=[jax.ShapeDtypeStruct(*one) for...  19.8 us
    pallas_call x1, Pallas kernels, per_device(): pl.pallas_call(store_kernel, out_shape=out_shape, in_specs=[vmem] * 4, ou...  1.11 us

profile of v6, /device:TPU:6, one launch (start us, length us, event | category | flops | bytes accessed | tf_op | source)
XLA Modules:
  0.0 47.3 jit_solution(1110141350217306955)
XLA Ops:
  0.6 19.8 %shard_map.129 = (bf16[1024,512]{1,0:T(8,128)(2,1)S(1)}, bf16[1024,512]{1,0:T(8,128)(2,1)S(1)}, bf16[42,8192]{1,0:T(8,128)(2,1)S(1)}, bf16[64,512]{1,0:T(8,128)(...) custom-call(bf16[1024,512]{1,0:T(8,128)(2,1)} %edge_hbm.1, ...), custom_call_target="tpu_custom_call" | custom-call | tf_op jit(solution)/shard_map/pallas_call | solution.py:605
  20.4 25.8 %shard_map.130 = (bf16[1024,512]{1,0:T(8,128)(2,1)S(1)}, f32[64,512]{1,0:T(8,128)S(1)}, f32[42,64]{1,0:T(8,128)S(1)}, f32[64,512]{1,0:T(8,128)S(1)}) custom-call(bf16[1024,512]{1,0:T(8,128)(2,1)S(1)} %get-tuple-element.28.edge, bf16[1024,512]{1,0:T(8,128)(2,1)S(1)} %get-tuple-element.29.cot, bf16[42,8192]{1,0:T(8,128)(2,1)S(1)} %get-tuple-element.30.bv, ...), custom_call_target="tpu_custom_call" | custom-call | tf_op jit(solution)/shard_map/pallas_call | solution.py:631
  46.2 1.1 %shard_map.131 = (bf16[1024,512]{1,0:T(8,128)(2,1)}, f32[64,512]{1,0:T(8,128)}, f32[42,64]{1,0:T(8,128)}, f32[64,512]{1,0:T(8,128)}) custom-call(bf16[1024,512]{1,0:T(8,128)(2,1)S(1)} %get-tuple-element.44.a, f32[64,512]{1,0:T(8,128)S(1)} %get-tuple-element.45.b, f32[42,64]{1,0:T(8,128)S(1)} %get-tuple-element.46.c, f32[64,512]{1,0:T(8,128)S(1)} %get-tuple-element.47.d), custom_call_target="tpu_custom_call" | custom-call | tf_op jit(solution)/shard_map/pallas_call | solution.py:654
